TPU v7x, 256 devices: a whole 4x4x8 slice. The times are simulated.
256 devices in a mesh: view: 8 (over z_hi, core), gz: 32 (over z_lo, y, x).
Axes of the slice: x: 4, y: 4, z: 8 (z_hi: 4, z_lo: 2; z = z_hi * 2 + z_lo), core: 2. Of those that a mesh axis runs over, the one named last changes fastest.
Arguments:
- estimate: float32 [1536, 128, 128], P('gz'), may hold values from 0.5 to 2
- measured: float32 [8, 1536, 128, 128], P('view', 'gz'), may hold values from 0.3 to 3
- lateral_x: float32 [8, 128, 128], P('view'), may hold values from 0 to 0.5, as said below
- lateral_y: float32 [8, 128, 128], P('view'), may hold values from 0 to 0.5, as said below
- depth_taps: float32 [8, 33], P('view'), may hold values from 0.01 to 0.06
Outputs:
- updated: float32 [1536, 128, 128], P('gz')
Inputs may be any that keep to these rules, and one draw needn't show every extreme that they name: `lateral_x`: nonnegative entries. `lateral_y`: nonnegative entries.
All inputs are finite; a program needn't handle non-finite values.
Results may differ from a plain program's by a relative error of at most 0.0001.
Values sent between devices are 32-bit elements; how exact they have to be, the bound alone decides.
No kernel may reach another device: no remote copies, remote signals or barrier semaphores. Data moves between devices by JAX's collectives and lax.ppermute only.
A program may use at most 64 MiB of HBM per device.

v0:
```python
import jax
import jax.numpy as jnp
from jax import lax
from jax.experimental import pallas as pl
from jax.experimental.pallas import tpu as pltpu
from jax.sharding import PartitionSpec as P

DEPTH = 33
HALF = 16
N = 128
SLAB = 48
FAR = 2 * HALF
F32 = jnp.float32
BF16 = jnp.bfloat16
MIB = 1024 * 1024
PITCH = 132
STEP = 16
LOTS = (1, 2)


def split(x):
    hi = x.astype(BF16)
    return hi, (x - hi.astype(F32)).astype(BF16)


def left_product(operand, x):
    hi, lo = split(x)
    out = jnp.dot(operand, jnp.concatenate([hi, lo], 0), preferred_element_type=F32)
    rows = operand.shape[0] // 2
    return out[:rows] + out[rows:]


def right_product(x, operand):
    hi, lo = split(x)
    out = jnp.dot(jnp.concatenate([hi, lo], 1), operand, preferred_element_type=F32)
    cols = operand.shape[1] // 2
    return out[:, :cols] + out[:, cols:]


def two_sided(planes, left, right):
    sides = [
        left_product(left, jnp.concatenate(planes[i : i + 2], 1)) for i in range(0, len(planes), 2)
    ]
    rows = jnp.concatenate([part for s in sides for part in (s[:, :N], s[:, N:])], 0)
    return right_product(rows, right)


def region_plane(refs, z):
    blocks = []
    for ref in refs:
        if len(ref.shape) == 3:
            blocks.append(ref[z])
        else:
            blocks.extend(ref[p, z] for p in range(ref.shape[0]))
    return jnp.concatenate(blocks, 0) if len(blocks) > 1 else blocks[0]


def lateral_kernel(counts, *refs):
    total = sum(c for c, _ in counts)
    ins, (left_ref, right_ref), outs = refs[:total], refs[total : total + 2], refs[total + 2 :]
    left = left_ref[...]
    right = right_ref[...]
    at = 0
    for (count, planes), out in zip(counts, outs):
        region = ins[at : at + count]
        at += count

        @pl.loop(0, planes // STEP)
        def _(i, region=region, out=out):
            zs = [STEP * i + j for j in range(STEP)]
            res = two_sided([region_plane(region, z) for z in zs], left, right)
            for j, z in enumerate(zs):
                out[pl.ds(z * PITCH, N), :] = res[j * N : j * N + N]


def lateral(regions, left, right):
    counts = []
    ins = []
    for region in regions:
        ref = region[0]
        counts.append((len(region), ref.shape[0] if ref.ndim == 3 else ref.shape[1]))
        ins.extend(region)
    planes = sum(p for _, p in counts)
    return pl.pallas_call(
        lambda *refs: lateral_kernel(counts, *refs),
        out_shape=[jax.ShapeDtypeStruct((p * PITCH, N), F32) for _, p in counts],
        in_specs=[pl.BlockSpec(memory_space=pltpu.VMEM)] * (len(ins) + 2),
        out_specs=[pl.BlockSpec(memory_space=pltpu.VMEM)] * len(counts),
        compiler_params=pltpu.CompilerParams(vmem_limit_bytes=24 * MIB),
        cost_estimate=pl.CostEstimate(flops=planes * 16 * N**3, bytes_accessed=planes * 8 * N * N, transcendentals=0),
        name="lateral",
    )(*ins, left, right)


def strided(refs, a):
    return jnp.concatenate([r[pl.ds(a, r.shape[0] // PITCH, stride=PITCH), :] for r in refs], 0)


def at_row(refs, a):
    return jnp.concatenate([r[a] for r in refs], 0)


def pair(pick, refs, a):
    return jnp.concatenate([pick(refs, a), pick(refs, a + 1)], 1)


def store_back(back, a, res):
    back[pl.ds(a, SLAB, stride=PITCH), :] = res[:, :N]
    back[pl.ds(a + 1, SLAB, stride=PITCH), :] = res[:, N:]


def logs_out(back, left_ref, right_ref, owns, others):
    left = left_ref[...]
    right = right_ref[...]
    begin = 0
    for own, other in zip(owns, others):
        planes = own.shape[1]
        step = 16 if planes % 16 == 0 else 8

        @pl.loop(0, planes // step)
        def _(i, own=own, other=other, begin=begin, step=step):
            zs = [step * i + j for j in range(step)]
            sides = [back[pl.ds((begin + z) * PITCH, N), :] for z in zs]
            logs = jnp.log(two_sided(sides, left, right))
            for j, z in enumerate(zs):
                for p in range(8):
                    own[p, z] = logs[j * N + 8 * p : j * N + 8 * p + 8]
                    other[p, z] = logs[j * N + 64 + 8 * p : j * N + 64 + 8 * p + 8]

        begin += planes


def middle_kernel(sb, so, sa, mb, mo, ma, tf_ref, ta_ref, left_ref, right_ref, *outs):
    outs, back = outs[:-1], outs[-1]
    lots = len(outs) // 2
    tf = tf_ref[...]
    ta = ta_ref[...]

    @pl.loop(0, N // STEP)
    def _(i):
        firsts = [STEP * i + j for j in range(0, STEP, 2)]
        blurred = [left_product(tf, pair(strided, (sb, so, sa), a)) for a in firsts]
        ratios = []
        for a, blur in zip(firsts, blurred):
            rec = pair(at_row, (mb, mo, ma), a)
            ratios.append(jnp.where(rec > 0, rec / blur, 0.0))
        for a, ratio in zip(firsts, ratios):
            store_back(back, a, left_product(ta, ratio))

    logs_out(back, left_ref, right_ref, outs[:lots], outs[lots:])


def middle(lots, smooth, recorded, tf, ta, left, right):
    ins = (*smooth, *recorded, tf, ta, left, right)
    half = jax.ShapeDtypeStruct((8, SLAB // lots, 8, N), F32)
    res = pl.pallas_call(
        middle_kernel,
        out_shape=[half] * (2 * lots),
        in_specs=[pl.BlockSpec(memory_space=pltpu.VMEM)] * len(ins),
        out_specs=[pl.BlockSpec(memory_space=pltpu.VMEM)] * (2 * lots),
        scratch_shapes=[pltpu.VMEM((SLAB * PITCH, N), F32)],
        compiler_params=pltpu.CompilerParams(vmem_limit_bytes=32 * MIB),
        cost_estimate=pl.CostEstimate(flops=8 * 10**9, bytes_accessed=15 * MIB, transcendentals=SLAB * N * N),
        name="middle",
    )(*ins)
    return res[:lots], res[lots:]


def operand_rows(m):
    hi, lo = split(m)
    return jnp.concatenate([hi, lo], 0)


def twice(m, axis):
    return jnp.concatenate([m, m], axis)


def operand_cols(m):
    hi, lo = split(twice(m, 0))
    return jnp.concatenate([hi, lo], 1)


def prep_kernel(
    starts, taps, mx_ref, my_ref, rec,
    tf, ta, x_all, x_halves, x_pieces, adj_x, fwd_y, adj_y, rec_t, rec_first, rec_last, xt_ref,
):
    def toeplitz(rows, cols, flip):
        i = lax.broadcasted_iota(jnp.int32, (rows, 2 * cols), 0)
        j = lax.broadcasted_iota(jnp.int32, (rows, 2 * cols), 1)
        diag = jnp.where(j >= cols, j - cols, j) - i
        out = jnp.zeros((rows, 2 * cols), F32)
        for k in range(DEPTH):
            out = jnp.where(diag == k, taps[0, DEPTH - 1 - k if flip else k], out)
        return out

    tf[...] = operand_rows(toeplitz(SLAB + 2 * HALF, SLAB + 2 * FAR, False))
    ta[...] = operand_rows(toeplitz(SLAB, SLAB + 2 * HALF, True))
    mx = mx_ref[...]
    my = my_ref[...]
    x_all[...] = operand_rows(twice(mx, 1))
    fwd_y[...] = operand_cols(my.T)
    adj_y[...] = operand_cols(my)
    xt_ref[...] = mx.T

    def row_blocks(rows):
        return jnp.concatenate([xt_ref[pl.ds(pl.multiple_of(r, 8), 8), :] for r in rows], 0)

    pieces = row_blocks([starts[p] for p in range(16)])
    adj_x[...] = operand_rows(twice(pieces, 1))
    x_pieces[...] = operand_rows(twice(pieces.T, 1))
    core = starts[16]
    halves = row_blocks([core * 64 + 8 * p for p in range(8)] + [64 - core * 64 + 8 * p for p in range(8)])
    x_halves[...] = operand_rows(twice(halves.T, 1))

    @pl.loop(0, N // 8)
    def _(i):
        at = pl.multiple_of(8 * i, 8)
        for zb in range(0, SLAB, 8):
            block = jnp.stack([rec[z, pl.ds(at, 8), :] for z in range(zb, zb + 8)], 0)
            block = jnp.swapaxes(block, 0, 1)
            for j in range(8):
                rec_t[at + j, zb : zb + 8, :] = block[j]
                if zb < HALF:
                    rec_first[at + j, zb : zb + 8, :] = block[j]
                if zb >= SLAB - HALF:
                    rec_last[at + j, zb - SLAB + HALF : zb - SLAB + HALF + 8, :] = block[j]


def prep(starts, taps, mx, my, rec):
    full = SLAB + 2 * HALF
    wide = SLAB + 2 * FAR
    square = jax.ShapeDtypeStruct((2 * N, 2 * N), BF16)
    edge = jax.ShapeDtypeStruct((N, HALF, N), F32)
    outs = [
        jax.ShapeDtypeStruct((2 * full, 2 * wide), BF16),
        jax.ShapeDtypeStruct((2 * SLAB, 2 * full), BF16),
        *[square] * 6,
        jax.ShapeDtypeStruct((N, SLAB, N), F32),
        edge,
        edge,
    ]
    vmem = pl.BlockSpec(memory_space=pltpu.VMEM)
    smem = pl.BlockSpec(memory_space=pltpu.SMEM)
    return pl.pallas_call(
        prep_kernel,
        out_shape=outs,
        in_specs=[smem, smem, vmem, vmem, vmem],
        out_specs=[vmem] * len(outs),
        scratch_shapes=[pltpu.VMEM((N, N), F32)],
        compiler_params=pltpu.CompilerParams(vmem_limit_bytes=20 * MIB),
        name="prep",
    )(starts, taps, mx, my, rec)


def place_kernel(lots, starts, *refs):
    out = refs[-1]
    per = (len(refs) - 1) // lots
    for k in range(lots):
        at = 0
        for ref in refs[k * per : k * per + per]:
            planes = ref.shape[1]
            for p in range(ref.shape[0]):
                begin = pl.multiple_of(starts[at], 8)
                out[k * planes : (k + 1) * planes, pl.ds(begin, 8), :] = ref[p]
                at += 1


def place(starts, lots):
    pieces = [p for lot in lots for p in lot]
    return pl.pallas_call(
        lambda *refs: place_kernel(len(lots), *refs),
        out_shape=jax.ShapeDtypeStruct((SLAB, N, N), F32),
        in_specs=[pl.BlockSpec(memory_space=pltpu.SMEM)] + [pl.BlockSpec(memory_space=pltpu.VMEM)] * len(pieces),
        out_specs=pl.BlockSpec(memory_space=pltpu.VMEM),
        compiler_params=pltpu.CompilerParams(vmem_limit_bytes=4 * MIB),
        name="place",
    )(starts, *pieces)


def to_core(x):
    return lax.ppermute(x, "view", [(i, i ^ 1) for i in range(8)])


def to_next(x):
    return lax.ppermute(x, "view", [(i, (i + 2) % 8) for i in range(8)])


def to_prev(x):
    return lax.ppermute(x, "view", [(i, (i - 2) % 8) for i in range(8)])


def up(x):
    n = lax.axis_size("gz")
    return lax.ppermute(x, "gz", [(i, i + 1) for i in range(n - 1)])


def down(x):
    n = lax.axis_size("gz")
    return lax.ppermute(x, "gz", [(i + 1, i) for i in range(n - 1)])


def reduce_chunk(other, own):
    total = own + to_core(other)
    from_prev = to_next(total[0:2])
    from_next = to_prev(total[2:4])
    from_prev, from_next = lax.optimization_barrier((from_prev, from_next))
    fwd_next = total[4:5] + from_prev[0:1]
    fwd_prev = total[5:6] + from_next[0:1]
    fwd_next, fwd_prev = lax.optimization_barrier((fwd_next, fwd_prev))
    last_a = to_next(fwd_next)
    last_b = to_prev(fwd_prev)
    last_a, last_b = lax.optimization_barrier((last_a, last_b))
    a = total[6:7] + from_next[1:2] + last_a
    b = total[7:8] + from_prev[1:2] + last_b
    return jnp.concatenate([a, b], 0)


def on_device(estimate, measured, lateral_x, lateral_y, depth_taps):
    view = lax.axis_index("view")
    core = lax.rem(view, 2)
    chip = lax.div(view, 2)
    recorded = measured[0]
    mx = lateral_x[0]
    my = lateral_y[0]

    nxt, prv, opp = (chip + 1) % 4, (chip + 3) % 4, (chip + 2) % 4
    order = jnp.stack([2 * opp, 2 * nxt + 1, 2 * opp + 1, 2 * prv, 2 * nxt, 2 * prv + 1, 2 * chip, 2 * chip + 1])
    starts = jnp.concatenate([core * 64 + 8 * order, (1 - core) * 64 + 8 * order, core[None]]).astype(jnp.int32)

    before = up(lax.dynamic_slice(estimate, (SLAB - FAR, core * 64, 0), (FAR, 64, N)))
    after = down(lax.dynamic_slice(estimate, (0, core * 64, 0), (FAR, 64, N)))
    tf, ta, x_all, x_halves, x_fwd, adj_x, fwd_y, adj_y, rec_own, rec_first, rec_last = prep(
        starts, depth_taps, mx, my, recorded
    )
    before, after, rec_first, rec_last = lax.optimization_barrier((before, after, rec_first, rec_last))
    rec_before = up(rec_last)
    rec_after = down(rec_first)
    before2, after2 = to_core(before), to_core(after)

    def log_sums(update, smooth):
        recs = (rec_before, rec_own, rec_after)
        owns, others = middle(LOTS[update], smooth, recs, tf, ta, adj_x, adj_y)
        return [reduce_chunk(other, own) for own, other in zip(owns, others)]

    mine = lax.dynamic_slice(estimate, (0, core * 64 + chip * 16, 0), (SLAB, 16, N))
    mine = jnp.stack([mine[:, :8], mine[:, 8:]], 0)

    (smooth_own,) = lateral([[estimate]], x_all, fwd_y)
    smooth_b, smooth_a = lateral([[before, before2], [after, after2]], x_halves, fwd_y)
    (log_sum,) = log_sums(0, (smooth_b, smooth_own, smooth_a))
    mine = mine * jnp.exp(log_sum / 8.0)

    prev_c, next_c = to_next(mine), to_prev(mine)
    b0, a0 = up(mine[:, SLAB - FAR :]), down(mine[:, :FAR])
    opp_a, opp_b = to_next(prev_c[0:1]), to_prev(next_c[1:2])
    sides = jnp.concatenate([prev_c, next_c], 0)
    b1, a1 = up(sides[:, SLAB - FAR :]), down(sides[:, :FAR])
    near = jnp.concatenate([mine, sides], 0)
    near2 = to_core(near)
    opp_c = jnp.concatenate([opp_a, opp_b], 0)
    b2, a2 = up(opp_c[:, SLAB - FAR :]), down(opp_c[:, :FAR])
    opp2 = to_core(opp_c)
    ends = jnp.concatenate([b0, b1, a0, a1], 0)
    ends2 = to_core(ends)
    tail = jnp.concatenate([b2, a2], 0)
    tail2 = to_core(tail)

    def in_order(near, opp_c):
        mine, prv, nxt = near[0:2], near[2:4], near[4:6]
        return [opp_c[0:1], nxt[1:2], opp_c[1:2], prv[0:1], nxt[0:1], prv[1:2], mine]

    (smooth_own,) = lateral([in_order(near, opp_c) + in_order(near2, opp2)], x_fwd, fwd_y)
    smooth_b, smooth_a = lateral(
        [
            in_order(ends[0:6], tail[0:2]) + in_order(ends2[0:6], tail2[0:2]),
            in_order(ends[6:12], tail[2:4]) + in_order(ends2[6:12], tail2[2:4]),
        ],
        x_fwd,
        fwd_y,
    )
    lots = []
    for k, log_sum in enumerate(log_sums(1, (smooth_b, smooth_own, smooth_a))):
        planes = log_sum.shape[1]
        chunk = mine[:, k * planes : (k + 1) * planes] * jnp.exp(log_sum / 8.0)
        prev_c, next_c = lax.optimization_barrier((to_next(chunk), to_prev(chunk)))
        opp_a, opp_b = to_next(prev_c[0:1]), to_prev(next_c[1:2])
        ours = jnp.concatenate([opp_a, next_c[1:2], opp_b, prev_c[0:1], next_c[0:1], prev_c[1:2], chunk], 0)
        lots.append([ours, to_core(ours)])
    return place(starts, lots)


def solution(mesh):
    return jax.shard_map(
        on_device,
        mesh=mesh,
        in_specs=(
            P("gz", None, None),
            P("view", "gz", None, None),
            P("view", None, None),
            P("view", None, None),
            P("view", None),
        ),
        out_specs=P("gz", None, None),
        check_vma=False,
    )
```

profile of v0, /device:TPU:33, one launch (start us, length us, event | category | flops | bytes accessed | tf_op | source)
XLA Modules:
  0.0 261.6 jit_solution(17568269680254226167)
XLA Ops:
  0.0 3.1 %constant_dynamic-slice_fusion = (f32[32,64,128]{2,1,0:T(8,128)}, f32[32,64,128]{2,1,0:T(8,128)}) fusion(f32[48,128,128]{2,1,0:T(8,128)} %refs_0_.1, s32[]{:T(128)S(6)} %select_n.26), kind=kLoop, calls=%fused_computation.50 | loop fusion | bytes 4194308 | tf_op jit(solution)/shard_map/dynamic_slice | solution.py:331
  3.1 3.1 %collective-permute-start = (f32[32,64,128]{2,1,0:T(8,128)}, f32[32,64,128]{2,1,0:T(8,128)}, u32[]{:S(2)}, u32[]{:S(2)}) collective-permute-start(f32[32,64,128]{2,1,0:T(8,128)} %get-tuple-element.100), channel_id=1, source_target_pairs={{0,1},{1,2},{2,3},{3,4},{4,5},{5,6},{6,7},{7,8},{8,9},{9,10},{10,1... | collective-permute-start | bytes 3145736 | tf_op jit(solution)/shard_map/ppermute | solution.py:294
  6.3 6.4 %collective-permute-start.1 = (f32[32,64,128]{2,1,0:T(8,128)}, f32[32,64,128]{2,1,0:T(8,128)}, u32[]{:S(2)}, u32[]{:S(2)}) collective-permute-start(f32[32,64,128]{2,1,0:T(8,128)} %get-tuple-element.99), channel_id=1, source_target_pairs={{1,0},{2,1},{3,2},{4,3},{5,4},{6,5},{7,6},{8,7},{9,8},{10,9},{11,1... | collective-permute-start | bytes 3145736 | tf_op jit(solution)/shard_map/ppermute | solution.py:299
  16.5 17.0 %collective-permute-done.refs_0_ = f32[32,64,128]{2,1,0:T(8,128)} collective-permute-done((f32[32,64,128]{2,1,0:T(8,128)}, f32[32,64,128]{2,1,0:T(8,128)}, u32[]{:S(2)}, u32[]{:S(2)}) %collective-permute-start) | collective-permute-done | bytes 1048608 | tf_op jit(solution)/shard_map/ppermute | solution.py:294
  38.2 8.3 %collective-permute-start.5 = (f32[128,16,128]{2,1,0:T(8,128)S(1)}, f32[128,16,128]{2,1,0:T(8,128)S(1)}, u32[]{:S(2)}, u32[]{:S(2)}) collective-permute-start(f32[128,16,128]{2,1,0:T(8,128)S(1)} %get-tuple-element.63), channel_id=1, source_target_pairs={{1,0},{2,1},{3,2},{4,3},{5,4},{6,5},{7,6},{8,7},{9,8},{10,9},{11,1... | collective-permute-start | bytes 3145736 | tf_op jit(solution)/shard_map/ppermute | solution.py:299
  46.6 2.3 lateral.5.so
  48.9 4.5 %lateral.4 = (f32[4224,128]{1,0:T(8,128)S(1)}, f32[4224,128]{1,0:T(8,128)S(1)}) custom-call(f32[32,64,128]{2,1,0:T(8,128)} %collective-permute-done.refs_0_, f32[32,64,128]{2,1,0:T(8,128)S(1)} %collective-permute-done.2.refs_1_, f32[32,64,128]{2,1,0:T(8,128)} %collective-permute-done.1.refs_2_, f32[32,64,128]{2,1,0:T(8,128)S(1)} %collective-permute-done.3.refs_3_, ...), custom_call_target="tpu_custom_call" | custom-call | flops 2147483648 | bytes 8388608 | tf_op jit(solution)/shard_map/lateral/pallas_call | solution.py:84
  53.4 14.3 %collective-permute-done.4.mb = f32[128,16,128]{2,1,0:T(8,128)S(1)} collective-permute-done((f32[128,16,128]{2,1,0:T(8,128)S(1)}, f32[128,16,128]{2,1,0:T(8,128)S(1)}, u32[]{:S(2)}, u32[]{:S(2)}) %collective-permute-start.4) | collective-permute-done | bytes 1048608 | tf_op jit(solution)/shard_map/ppermute | solution.py:294
  68.6 6.6 %middle.2 = (f32[8,48,8,128]{3,2,1,0:T(8,128)S(1)}, f32[8,48,8,128]{3,2,1,0:T(8,128)S(1)}) custom-call(f32[4224,128]{1,0:T(8,128)S(1)} %get-tuple-element.58.sb, f32[6336,128]{1,0:T(8,128)S(1)} %lateral.5.so, f32[4224,128]{1,0:T(8,128)S(1)} %get-tuple-element.60.sa, f32[128,16,128]{2,1,0:T(8,128)S(1)} %collective-permute-done.4.mb, ...), custom_call_target="tpu_custom_call" | custom-call | flops 8000000000 | bytes 15728640 | tf_op jit(solution)/shard_map/middle/pallas_call | solution.py:156
  76.7 3.0 %collective-permute-done.6 = f32[8,48,8,128]{3,2,1,0:T(8,128)S(1)} collective-permute-done((f32[8,48,8,128]{3,2,1,0:T(8,128)S(1)}, f32[8,48,8,128]{3,2,1,0:T(8,128)S(1)}, u32[]{:S(2)}, u32[]{:S(2)}) %collective-permute-start.6) | collective-permute-done | bytes 1572896 | tf_op jit(solution)/shard_map/ppermute | solution.py:281
  80.0 3.1 %collective-permute-start.7 = (f32[2,48,8,128]{3,2,1,0:T(8,128)S(1)}, f32[2,48,8,128]{3,2,1,0:T(8,128)S(1)}, u32[]{:S(2)}, u32[]{:S(2)}) collective-permute-start(f32[2,48,8,128]{3,2,1,0:T(8,128)S(1)} %get-tuple-element.118), channel_id=1, source_target_pairs={{0,64},{32,96},{64,128},{96,160},{128,192},{160,224},{192,0},{224,... | collective-permute-start | bytes 1179656 | tf_op jit(solution)/shard_map/ppermute | solution.py:285
  83.1 2.2 collective-permute-start.8
  85.3 13.3 %collective-permute-done.7 = f32[2,48,8,128]{3,2,1,0:T(8,128)S(1)} collective-permute-done((f32[2,48,8,128]{3,2,1,0:T(8,128)S(1)}, f32[2,48,8,128]{3,2,1,0:T(8,128)S(1)}, u32[]{:S(2)}, u32[]{:S(2)}) %collective-permute-start.7) | collective-permute-done | bytes 393248 | tf_op jit(solution)/shard_map/ppermute | solution.py:285
  98.5 3.2 %collective-permute-done.8 = f32[2,48,8,128]{3,2,1,0:T(8,128)S(1)} collective-permute-done((f32[2,48,8,128]{3,2,1,0:T(8,128)S(1)}, f32[2,48,8,128]{3,2,1,0:T(8,128)S(1)}, u32[]{:S(2)}, u32[]{:S(2)}) %collective-permute-start.8) | collective-permute-done | bytes 393248 | tf_op jit(solution)/shard_map/ppermute | solution.py:289
  102.9 3.3 %collective-permute-start.10 = (f32[1,48,8,128]{3,2,1,0:T(8,128)}, f32[1,48,8,128]{3,2,1,0:T(8,128)}, u32[]{:S(2)}, u32[]{:S(2)}) collective-permute-start(f32[1,48,8,128]{3,2,1,0:T(8,128)} %get-tuple-element.73), channel_id=1, source_target_pairs={{0,192},{32,224},{64,0},{96,32},{128,64},{160,96},{192,128},{224,1... | collective-permute-start | bytes 589832 | tf_op jit(solution)/shard_map/ppermute | solution.py:289
  106.3 4.8 %collective-permute-done.9 = f32[1,48,8,128]{3,2,1,0:T(8,128)} collective-permute-done((f32[1,48,8,128]{3,2,1,0:T(8,128)}, f32[1,48,8,128]{3,2,1,0:T(8,128)}, u32[]{:S(2)}, u32[]{:S(2)}) %collective-permute-start.9) | collective-permute-done | bytes 196640 | tf_op jit(solution)/shard_map/ppermute | solution.py:285
  111.2 2.0 collective-permute-done.10
  115.7 3.1 %collective-permute-start.13 = (f32[2,48,8,128]{3,2,1,0:T(8,128)S(1)}, f32[2,48,8,128]{3,2,1,0:T(8,128)S(1)}, u32[]{:S(2)}, u32[]{:S(2)}) collective-permute-start(f32[2,48,8,128]{3,2,1,0:T(8,128)S(1)} %maximum_multiply_fusion.refs_6_), channel_id=1, source_target_pairs={{0,192},{32,224},{64,0},{96,32},{128,64},{160,96},{192,128},{224,1... | collective-permute-start | bytes 1179656 | tf_op jit(solution)/shard_map/ppermute | solution.py:289
  118.9 10.8 %collective-permute-done.11 = f32[2,48,8,128]{3,2,1,0:T(8,128)S(1)} collective-permute-done((f32[2,48,8,128]{3,2,1,0:T(8,128)S(1)}, f32[2,48,8,128]{3,2,1,0:T(8,128)S(1)}, u32[]{:S(2)}, u32[]{:S(2)}) %collective-permute-start.11) | collective-permute-done | bytes 393248 | tf_op jit(solution)/shard_map/ppermute | solution.py:285
  130.0 3.1 %collective-permute-done.13 = f32[2,48,8,128]{3,2,1,0:T(8,128)S(1)} collective-permute-done((f32[2,48,8,128]{3,2,1,0:T(8,128)S(1)}, f32[2,48,8,128]{3,2,1,0:T(8,128)S(1)}, u32[]{:S(2)}, u32[]{:S(2)}) %collective-permute-start.13) | collective-permute-done | bytes 393248 | tf_op jit(solution)/shard_map/ppermute | solution.py:289
  134.8 1.9 collective-permute-start.16
  136.7 7.6 %collective-permute-start.21 = (f32[4,32,8,128]{3,2,1,0:T(8,128)S(1)}, f32[4,32,8,128]{3,2,1,0:T(8,128)S(1)}, u32[]{:S(2)}, u32[]{:S(2)}) collective-permute-start(f32[4,32,8,128]{3,2,1,0:T(8,128)S(1)} %get-tuple-element.135), channel_id=1, source_target_pairs={{1,0},{2,1},{3,2},{4,3},{5,4},{6,5},{7,6},{8,7},{9,8},{10,9},{11,1... | collective-permute-start | bytes 1572872 | tf_op jit(solution)/shard_map/ppermute | solution.py:299
  144.4 1.9 collective-permute-start.15
  146.3 7.6 %collective-permute-start.18 = (f32[2,32,8,128]{3,2,1,0:T(8,128)S(1)}, f32[2,32,8,128]{3,2,1,0:T(8,128)S(1)}, u32[]{:S(2)}, u32[]{:S(2)}) collective-permute-start(f32[2,32,8,128]{3,2,1,0:T(8,128)S(1)} %get-tuple-element.159), channel_id=1, source_target_pairs={{1,0},{2,1},{3,2},{4,3},{5,4},{6,5},{7,6},{8,7},{9,8},{10,9},{11,1... | collective-permute-start | bytes 786440 | tf_op jit(solution)/shard_map/ppermute | solution.py:299
  154.0 1.9 collective-permute-start.17
  156.0 2.9 %collective-permute-done.15 = f32[2,32,8,128]{3,2,1,0:T(8,128)S(1)} collective-permute-done((f32[2,32,8,128]{3,2,1,0:T(8,128)S(1)}, f32[2,32,8,128]{3,2,1,0:T(8,128)S(1)}, u32[]{:S(2)}, u32[]{:S(2)}) %collective-permute-start.15) | collective-permute-done | bytes 262176 | tf_op jit(solution)/shard_map/ppermute | solution.py:294
  158.9 4.7 %collective-permute-start.20 = (f32[2,32,8,128]{3,2,1,0:T(8,128)S(1)}, f32[2,32,8,128]{3,2,1,0:T(8,128)S(1)}, u32[]{:S(2)}, u32[]{:S(2)}) collective-permute-start(f32[2,32,8,128]{3,2,1,0:T(8,128)S(1)} %get-tuple-element.157), channel_id=1, source_target_pairs={{1,0},{2,1},{3,2},{4,3},{5,4},{6,5},{7,6},{8,7},{9,8},{10,9},{11,1... | collective-permute-start | bytes 786440 | tf_op jit(solution)/shard_map/ppermute | solution.py:299
  163.6 8.9 %collective-permute-start.24 = (f32[6,48,8,128]{3,2,1,0:T(8,128)S(1)}, f32[6,48,8,128]{3,2,1,0:T(8,128)S(1)}, u32[]{:S(2)}, u32[]{:S(2)}) collective-permute-start(f32[6,48,8,128]{3,2,1,0:T(8,128)S(1)} %pad_maximum_fusion.1), channel_id=1, source_target_pairs={{0,32},{32,0},{64,96},{96,64},{128,160},{160,128},{192,224},{224,1... | collective-permute-start | bytes 3538952 | tf_op jit(solution)/shard_map/ppermute | solution.py:281
  172.6 2.1 collective-permute-start.23
  177.9 2.3 lateral.7.so
  180.4 3.0 %lateral.6 = (f32[4224,128]{1,0:T(8,128)S(1)}, f32[4224,128]{1,0:T(8,128)S(1)}) custom-call(f32[1,32,8,128]{3,2,1,0:T(8,128)S(1)} %get-tuple-element.164.refs_0_, f32[1,32,8,128]{3,2,1,0:T(8,128)S(1)} %get-tuple-element.148.refs_1_, f32[1,32,8,128]{3,2,1,0:T(8,128)S(1)} %get-tuple-element.163.refs_2_, f32[1,32,8,128]{3,2,1,0:T(8,128)S(1)} %get-tuple-element.147.refs_3_, ...), custom_call_target="tpu_custom_call" | custom-call | flops 2147483648 | bytes 8388608 | tf_op jit(solution)/shard_map/lateral/pallas_call | solution.py:84
  183.5 7.6 %middle.3 = (f32[8,24,8,128]{3,2,1,0:T(8,128)S(1)}, f32[8,24,8,128]{3,2,1,0:T(8,128)S(1)}, f32[8,24,8,128]{3,2,1,0:T(8,128)S(1)}, f32[8,24,8,128]{3,2,1,0:T(8,128)S(1)}) custom-call(f32[4224,128]{1,0:T(8,128)S(1)} %get-tuple-element.77.sb, f32[6336,128]{1,0:T(8,128)S(1)} %lateral.7.so, f32[4224,128]{1,0:T(8,128)S(1)} %get-tuple-element.78.sa, ...), custom_call_target="tpu_custom_call" | custom-call | flops 8000000000 | bytes 15728640 | tf_op jit(solution)/shard_map/middle/pallas_call | solution.py:156
  193.7 3.6 %collective-permute-start.37 = (f32[2,24,8,128]{3,2,1,0:T(8,128)S(1)}, f32[2,24,8,128]{3,2,1,0:T(8,128)S(1)}, u32[]{:S(2)}, u32[]{:S(2)}) collective-permute-start(f32[2,24,8,128]{3,2,1,0:T(8,128)S(1)} %get-tuple-element.127), channel_id=1, source_target_pairs={{0,192},{32,224},{64,0},{96,32},{128,64},{160,96},{192,128},{224,1... | collective-permute-start | bytes 589832 | tf_op jit(solution)/shard_map/ppermute | solution.py:289
  197.5 3.6 %collective-permute-start.27 = (f32[2,24,8,128]{3,2,1,0:T(8,128)S(1)}, f32[2,24,8,128]{3,2,1,0:T(8,128)S(1)}, u32[]{:S(2)}, u32[]{:S(2)}) collective-permute-start(f32[2,24,8,128]{3,2,1,0:T(8,128)S(1)} %get-tuple-element.133), channel_id=1, source_target_pairs={{0,192},{32,224},{64,0},{96,32},{128,64},{160,96},{192,128},{224,1... | collective-permute-start | bytes 589832 | tf_op jit(solution)/shard_map/ppermute | solution.py:289
  201.1 2.0 collective-permute-done.36
  204.3 2.4 collective-permute-start.38
  208.0 2.2 collective-permute-done.26
  212.2 2.0 collective-permute-start.29
  214.2 2.6 collective-permute-done.28
  217.0 12.9 %collective-permute-start.30 = (f32[2,24,8,128]{3,2,1,0:T(8,128)S(1)}, f32[2,24,8,128]{3,2,1,0:T(8,128)S(1)}, u32[]{:S(2)}, u32[]{:S(2)}) collective-permute-start(f32[2,24,8,128]{3,2,1,0:T(8,128)S(1)} %get-tuple-element.150), channel_id=1, source_target_pairs={{0,64},{32,96},{64,128},{96,160},{128,192},{160,224},{192,0},{224,... | collective-permute-start | bytes 589832 | tf_op jit(solution)/shard_map/ppermute | solution.py:285
  229.8 2.4 collective-permute-start.40
  234.5 2.1 collective-permute-done.31
  236.6 2.5 collective-permute-start.32
  239.1 3.7 %collective-permute-done.41 = f32[2,24,8,128]{3,2,1,0:T(8,128)S(1)} collective-permute-done((f32[2,24,8,128]{3,2,1,0:T(8,128)S(1)}, f32[2,24,8,128]{3,2,1,0:T(8,128)S(1)}, u32[]{:S(2)}, u32[]{:S(2)}) %collective-permute-start.41) | collective-permute-done | bytes 196640 | tf_op jit(solution)/shard_map/ppermute | solution.py:289
  242.7 2.7 %collective-permute-start.42 = (f32[1,24,8,128]{3,2,1,0:T(8,128)S(1)}, f32[1,24,8,128]{3,2,1,0:T(8,128)S(1)}, u32[]{:S(2)}, u32[]{:S(2)}) collective-permute-start(f32[1,24,8,128]{3,2,1,0:T(8,128)S(1)} %slice.400), channel_id=1, source_target_pairs={{0,64},{32,96},{64,128},{96,160},{128,192},{160,224},{192,0},{224,... | collective-permute-start | bytes 294920 | tf_op jit(solution)/shard_map/ppermute | solution.py:285
  250.3 3.2 %collective-permute-start.34 = (f32[8,24,8,128]{3,2,1,0:T(8,128)S(1)}, f32[8,24,8,128]{3,2,1,0:T(8,128)S(1)}, u32[]{:S(2)}, u32[]{:S(2)}) collective-permute-start(f32[8,24,8,128]{3,2,1,0:T(8,128)S(1)} %constant_dynamic-update-slice_fusion.4.refs_1_), channel_id=1, source_target_pairs={{0,32},{32,0},{64,96},{96,64},{128,160},{160,128},{192,224},{224,1... | collective-permute-start | bytes 2359304 | tf_op jit(solution)/shard_map/ppermute | solution.py:281
  253.6 3.5 %collective-permute-start.44 = (f32[8,24,8,128]{3,2,1,0:T(8,128)S(1)}, f32[8,24,8,128]{3,2,1,0:T(8,128)S(1)}, u32[]{:S(2)}, u32[]{:S(2)}) collective-permute-start(f32[8,24,8,128]{3,2,1,0:T(8,128)S(1)} %constant_dynamic-update-slice_fusion.9.refs_3_), channel_id=1, source_target_pairs={{0,32},{32,0},{64,96},{96,64},{128,160},{160,128},{192,224},{224,1... | collective-permute-start | bytes 2359304 | tf_op jit(solution)/shard_map/ppermute | solution.py:281
  259.0 2.6 place.1
  (151 shorter events, 36.8 us)
Async XLA Ops:
  3.1 30.4 %collective-permute-start = (f32[32,64,128]{2,1,0:T(8,128)}, f32[32,64,128]{2,1,0:T(8,128)}, u32[]{:S(2)}, u32[]{:S(2)}) collective-permute-start(f32[32,64,128]{2,1,0:T(8,128)} %get-tuple-element.100), channel_id=1, source_target_pairs={{0,1},{1,2},{2,3},{3,4},{4,5},{5,6},{6,7},{7,8},{8,9},{9,10},{10,1... | collective-permute-start | bytes 3145736 | tf_op jit(solution)/shard_map/ppermute | solution.py:294
  6.3 28.2 %collective-permute-start.1 = (f32[32,64,128]{2,1,0:T(8,128)}, f32[32,64,128]{2,1,0:T(8,128)}, u32[]{:S(2)}, u32[]{:S(2)}) collective-permute-start(f32[32,64,128]{2,1,0:T(8,128)} %get-tuple-element.99), channel_id=1, source_target_pairs={{1,0},{2,1},{3,2},{4,3},{5,4},{6,5},{7,6},{8,7},{9,8},{10,9},{11,1... | collective-permute-start | bytes 3145736 | tf_op jit(solution)/shard_map/ppermute | solution.py:299
  16.5 52.1 %copy-start.5 = (f32[128,48,128]{2,1,0:T(8,128)}, f32[128,48,128]{2,1,0:T(8,128)S(1)}, u32[]{:S(2)}) copy-start(f32[128,48,128]{2,1,0:T(8,128)S(1)} %get-tuple-element.62.mo) | copy-start | bytes 9437188
  16.5 52.1 %copy-start.11 = (bf16[256,256]{1,0:T(8,128)(2,1)}, bf16[256,256]{1,0:T(8,128)(2,1)S(1)}, u32[]{:S(2)}) copy-start(bf16[256,256]{1,0:T(8,128)(2,1)S(1)} %get-tuple-element.66.left_ref) | copy-start | bytes 393220
  16.5 52.1 %copy-start.13 = (bf16[256,256]{1,0:T(8,128)(2,1)}, bf16[256,256]{1,0:T(8,128)(2,1)S(1)}, u32[]{:S(2)}) copy-start(bf16[256,256]{1,0:T(8,128)(2,1)S(1)} %get-tuple-element.67.right_ref) | copy-start | bytes 393220
  34.4 14.4 %collective-permute-start.2 = (f32[32,64,128]{2,1,0:T(8,128)}, f32[32,64,128]{2,1,0:T(8,128)S(1)}, u32[]{:S(2)}, u32[]{:S(2)}) collective-permute-start(f32[32,64,128]{2,1,0:T(8,128)} %collective-permute-done.refs_0_), channel_id=1, source_target_pairs={{0,32},{32,0},{64,96},{96,64},{128,160},{160,128},{192,224},{224,1... | collective-permute-start | bytes 3145736 | tf_op jit(solution)/shard_map/ppermute | solution.py:281
  36.3 12.5 %collective-permute-start.3 = (f32[32,64,128]{2,1,0:T(8,128)}, f32[32,64,128]{2,1,0:T(8,128)S(1)}, u32[]{:S(2)}, u32[]{:S(2)}) collective-permute-start(f32[32,64,128]{2,1,0:T(8,128)} %collective-permute-done.1.refs_2_), channel_id=1, source_target_pairs={{0,32},{32,0},{64,96},{96,64},{128,160},{160,128},{192,224},{224,1... | collective-permute-start | bytes 3145736 | tf_op jit(solution)/shard_map/ppermute | solution.py:281
  36.3 31.4 %collective-permute-start.4 = (f32[128,16,128]{2,1,0:T(8,128)S(1)}, f32[128,16,128]{2,1,0:T(8,128)S(1)}, u32[]{:S(2)}, u32[]{:S(2)}) collective-permute-start(f32[128,16,128]{2,1,0:T(8,128)S(1)} %get-tuple-element.61), channel_id=1, source_target_pairs={{0,1},{1,2},{2,3},{3,4},{4,5},{5,6},{6,7},{7,8},{8,9},{9,10},{10,1... | collective-permute-start | bytes 3145736 | tf_op jit(solution)/shard_map/ppermute | solution.py:294
  38.2 30.3 %collective-permute-start.5 = (f32[128,16,128]{2,1,0:T(8,128)S(1)}, f32[128,16,128]{2,1,0:T(8,128)S(1)}, u32[]{:S(2)}, u32[]{:S(2)}) collective-permute-start(f32[128,16,128]{2,1,0:T(8,128)S(1)} %get-tuple-element.63), channel_id=1, source_target_pairs={{1,0},{2,1},{3,2},{4,3},{5,4},{6,5},{7,6},{8,7},{9,8},{10,9},{11,1... | collective-permute-start | bytes 3145736 | tf_op jit(solution)/shard_map/ppermute | solution.py:299
  75.3 4.5 %collective-permute-start.6 = (f32[8,48,8,128]{3,2,1,0:T(8,128)S(1)}, f32[8,48,8,128]{3,2,1,0:T(8,128)S(1)}, u32[]{:S(2)}, u32[]{:S(2)}) collective-permute-start(f32[8,48,8,128]{3,2,1,0:T(8,128)S(1)} %get-tuple-element.69), channel_id=1, source_target_pairs={{0,32},{32,0},{64,96},{96,64},{128,160},{160,128},{192,224},{224,1... | collective-permute-start | bytes 4718600 | tf_op jit(solution)/shard_map/ppermute | solution.py:281
  80.0 18.6 %collective-permute-start.7 = (f32[2,48,8,128]{3,2,1,0:T(8,128)S(1)}, f32[2,48,8,128]{3,2,1,0:T(8,128)S(1)}, u32[]{:S(2)}, u32[]{:S(2)}) collective-permute-start(f32[2,48,8,128]{3,2,1,0:T(8,128)S(1)} %get-tuple-element.118), channel_id=1, source_target_pairs={{0,64},{32,96},{64,128},{96,160},{128,192},{160,224},{192,0},{224,... | collective-permute-start | bytes 1179656 | tf_op jit(solution)/shard_map/ppermute | solution.py:285
  83.1 18.7 %collective-permute-start.8 = (f32[2,48,8,128]{3,2,1,0:T(8,128)S(1)}, f32[2,48,8,128]{3,2,1,0:T(8,128)S(1)}, u32[]{:S(2)}, u32[]{:S(2)}) collective-permute-start(f32[2,48,8,128]{3,2,1,0:T(8,128)S(1)} %get-tuple-element.117), channel_id=1, source_target_pairs={{0,192},{32,224},{64,0},{96,32},{128,64},{160,96},{192,128},{224,1... | collective-permute-start | bytes 1179656 | tf_op jit(solution)/shard_map/ppermute | solution.py:289
  102.7 8.5 %collective-permute-start.9 = (f32[1,48,8,128]{3,2,1,0:T(8,128)}, f32[1,48,8,128]{3,2,1,0:T(8,128)}, u32[]{:S(2)}, u32[]{:S(2)}) collective-permute-start(f32[1,48,8,128]{3,2,1,0:T(8,128)} %get-tuple-element.72), channel_id=1, source_target_pairs={{0,64},{32,96},{64,128},{96,160},{128,192},{160,224},{192,0},{224,... | collective-permute-start | bytes 589832 | tf_op jit(solution)/shard_map/ppermute | solution.py:285
  102.9 10.2 %collective-permute-start.10 = (f32[1,48,8,128]{3,2,1,0:T(8,128)}, f32[1,48,8,128]{3,2,1,0:T(8,128)}, u32[]{:S(2)}, u32[]{:S(2)}) collective-permute-start(f32[1,48,8,128]{3,2,1,0:T(8,128)} %get-tuple-element.73), channel_id=1, source_target_pairs={{0,192},{32,224},{64,0},{96,32},{128,64},{160,96},{192,128},{224,1... | collective-permute-start | bytes 589832 | tf_op jit(solution)/shard_map/ppermute | solution.py:289
  114.6 15.1 %collective-permute-start.11 = (f32[2,48,8,128]{3,2,1,0:T(8,128)S(1)}, f32[2,48,8,128]{3,2,1,0:T(8,128)S(1)}, u32[]{:S(2)}, u32[]{:S(2)}) collective-permute-start(f32[2,48,8,128]{3,2,1,0:T(8,128)S(1)} %maximum_multiply_fusion.refs_6_), channel_id=1, source_target_pairs={{0,64},{32,96},{64,128},{96,160},{128,192},{160,224},{192,0},{224,... | collective-permute-start | bytes 1179656 | tf_op jit(solution)/shard_map/ppermute | solution.py:285
  115.7 17.3 %collective-permute-start.13 = (f32[2,48,8,128]{3,2,1,0:T(8,128)S(1)}, f32[2,48,8,128]{3,2,1,0:T(8,128)S(1)}, u32[]{:S(2)}, u32[]{:S(2)}) collective-permute-start(f32[2,48,8,128]{3,2,1,0:T(8,128)S(1)} %maximum_multiply_fusion.refs_6_), channel_id=1, source_target_pairs={{0,192},{32,224},{64,0},{96,32},{128,64},{160,96},{192,128},{224,1... | collective-permute-start | bytes 1179656 | tf_op jit(solution)/shard_map/ppermute | solution.py:289
  129.7 14.6 %collective-permute-start.12 = (f32[1,48,8,128]{3,2,1,0:T(8,128)S(1)}, f32[1,48,8,128]{3,2,1,0:T(8,128)S(1)}, u32[]{:S(2)}, u32[]{:S(2)}) collective-permute-start(f32[1,48,8,128]{3,2,1,0:T(8,128)S(1)} %get-tuple-element.154.refs_3_), channel_id=1, source_target_pairs={{0,64},{32,96},{64,128},{96,160},{128,192},{160,224},{192,0},{224,... | collective-permute-start | bytes 589832 | tf_op jit(solution)/shard_map/ppermute | solution.py:285
  133.1 11.2 %collective-permute-start.14 = (f32[1,48,8,128]{3,2,1,0:T(8,128)S(1)}, f32[1,48,8,128]{3,2,1,0:T(8,128)S(1)}, u32[]{:S(2)}, u32[]{:S(2)}) collective-permute-start(f32[1,48,8,128]{3,2,1,0:T(8,128)S(1)} %get-tuple-element.156.refs_1_), channel_id=1, source_target_pairs={{0,192},{32,224},{64,0},{96,32},{128,64},{160,96},{192,128},{224,1... | collective-permute-start | bytes 589832 | tf_op jit(solution)/shard_map/ppermute | solution.py:289
  134.8 41.5 %collective-permute-start.16 = (f32[4,32,8,128]{3,2,1,0:T(8,128)S(1)}, f32[4,32,8,128]{3,2,1,0:T(8,128)S(1)}, u32[]{:S(2)}, u32[]{:S(2)}) collective-permute-start(f32[4,32,8,128]{3,2,1,0:T(8,128)S(1)} %get-tuple-element.136), channel_id=1, source_target_pairs={{0,1},{1,2},{2,3},{3,4},{4,5},{5,6},{6,7},{7,8},{8,9},{9,10},{10,1... | collective-permute-start | bytes 1572872 | tf_op jit(solution)/shard_map/ppermute | solution.py:294
  136.7 39.6 %collective-permute-start.21 = (f32[4,32,8,128]{3,2,1,0:T(8,128)S(1)}, f32[4,32,8,128]{3,2,1,0:T(8,128)S(1)}, u32[]{:S(2)}, u32[]{:S(2)}) collective-permute-start(f32[4,32,8,128]{3,2,1,0:T(8,128)S(1)} %get-tuple-element.135), channel_id=1, source_target_pairs={{1,0},{2,1},{3,2},{4,3},{5,4},{6,5},{7,6},{8,7},{9,8},{10,9},{11,1... | collective-permute-start | bytes 1572872 | tf_op jit(solution)/shard_map/ppermute | solution.py:299
  144.4 14.5 %collective-permute-start.15 = (f32[2,32,8,128]{3,2,1,0:T(8,128)S(1)}, f32[2,32,8,128]{3,2,1,0:T(8,128)S(1)}, u32[]{:S(2)}, u32[]{:S(2)}) collective-permute-start(f32[2,32,8,128]{3,2,1,0:T(8,128)S(1)} %get-tuple-element.160), channel_id=1, source_target_pairs={{0,1},{1,2},{2,3},{3,4},{4,5},{5,6},{6,7},{7,8},{8,9},{9,10},{10,1... | collective-permute-start | bytes 786440 | tf_op jit(solution)/shard_map/ppermute | solution.py:294
  146.3 17.2 %collective-permute-start.18 = (f32[2,32,8,128]{3,2,1,0:T(8,128)S(1)}, f32[2,32,8,128]{3,2,1,0:T(8,128)S(1)}, u32[]{:S(2)}, u32[]{:S(2)}) collective-permute-start(f32[2,32,8,128]{3,2,1,0:T(8,128)S(1)} %get-tuple-element.159), channel_id=1, source_target_pairs={{1,0},{2,1},{3,2},{4,3},{5,4},{6,5},{7,6},{8,7},{9,8},{10,9},{11,1... | collective-permute-start | bytes 786440 | tf_op jit(solution)/shard_map/ppermute | solution.py:299
  154.0 18.6 %collective-permute-start.17 = (f32[2,32,8,128]{3,2,1,0:T(8,128)S(1)}, f32[2,32,8,128]{3,2,1,0:T(8,128)S(1)}, u32[]{:S(2)}, u32[]{:S(2)}) collective-permute-start(f32[2,32,8,128]{3,2,1,0:T(8,128)S(1)} %get-tuple-element.158), channel_id=1, source_target_pairs={{0,1},{1,2},{2,3},{3,4},{4,5},{5,6},{6,7},{7,8},{8,9},{9,10},{10,1... | collective-permute-start | bytes 786440 | tf_op jit(solution)/shard_map/ppermute | solution.py:294
  158.9 15.8 %collective-permute-start.20 = (f32[2,32,8,128]{3,2,1,0:T(8,128)S(1)}, f32[2,32,8,128]{3,2,1,0:T(8,128)S(1)}, u32[]{:S(2)}, u32[]{:S(2)}) collective-permute-start(f32[2,32,8,128]{3,2,1,0:T(8,128)S(1)} %get-tuple-element.157), channel_id=1, source_target_pairs={{1,0},{2,1},{3,2},{4,3},{5,4},{6,5},{7,6},{8,7},{9,8},{10,9},{11,1... | collective-permute-start | bytes 786440 | tf_op jit(solution)/shard_map/ppermute | solution.py:299
  163.6 14.3 %collective-permute-start.24 = (f32[6,48,8,128]{3,2,1,0:T(8,128)S(1)}, f32[6,48,8,128]{3,2,1,0:T(8,128)S(1)}, u32[]{:S(2)}, u32[]{:S(2)}) collective-permute-start(f32[6,48,8,128]{3,2,1,0:T(8,128)S(1)} %pad_maximum_fusion.1), channel_id=1, source_target_pairs={{0,32},{32,0},{64,96},{96,64},{128,160},{160,128},{192,224},{224,1... | collective-permute-start | bytes 3538952 | tf_op jit(solution)/shard_map/ppermute | solution.py:281
  172.6 4.0 %collective-permute-start.23 = (f32[2,48,8,128]{3,2,1,0:T(8,128)S(1)}, f32[2,48,8,128]{3,2,1,0:T(8,128)S(1)}, u32[]{:S(2)}, u32[]{:S(2)}) collective-permute-start(f32[2,48,8,128]{3,2,1,0:T(8,128)S(1)} %constant_dynamic-update-slice_fusion), channel_id=1, source_target_pairs={{0,32},{32,0},{64,96},{96,64},{128,160},{160,128},{192,224},{224,1... | collective-permute-start | bytes 1179656 | tf_op jit(solution)/shard_map/ppermute | solution.py:281
  174.7 3.1 %collective-permute-start.19 = (f32[4,32,8,128]{3,2,1,0:T(8,128)S(1)}, f32[4,32,8,128]{3,2,1,0:T(8,128)S(1)}, u32[]{:S(2)}, u32[]{:S(2)}) collective-permute-start(f32[4,32,8,128]{3,2,1,0:T(8,128)S(1)} %pad_maximum_fusion.2), channel_id=1, source_target_pairs={{0,32},{32,0},{64,96},{96,64},{128,160},{160,128},{192,224},{224,1... | collective-permute-start | bytes 1572872 | tf_op jit(solution)/shard_map/ppermute | solution.py:281
  176.4 3.8 %collective-permute-start.22 = (f32[12,32,8,128]{3,2,1,0:T(8,128)S(1)}, f32[12,32,8,128]{3,2,1,0:T(8,128)S(1)}, u32[]{:S(2)}, u32[]{:S(2)}) collective-permute-start(f32[12,32,8,128]{3,2,1,0:T(8,128)S(1)} %pad_maximum_fusion), channel_id=1, source_target_pairs={{0,32},{32,0},{64,96},{96,64},{128,160},{160,128},{192,224},{224,1... | collective-permute-start | bytes 4718600 | tf_op jit(solution)/shard_map/ppermute | solution.py:281
  191.1 2.4 collective-permute-start.35
  191.6 5.7 %collective-permute-start.25 = (f32[8,24,8,128]{3,2,1,0:T(8,128)S(1)}, f32[8,24,8,128]{3,2,1,0:T(8,128)S(1)}, u32[]{:S(2)}, u32[]{:S(2)}) collective-permute-start(f32[8,24,8,128]{3,2,1,0:T(8,128)S(1)} %get-tuple-element.80), channel_id=1, source_target_pairs={{0,32},{32,0},{64,96},{96,64},{128,160},{160,128},{192,224},{224,1... | collective-permute-start | bytes 2359304 | tf_op jit(solution)/shard_map/ppermute | solution.py:281
  193.6 9.4 %collective-permute-start.36 = (f32[2,24,8,128]{3,2,1,0:T(8,128)S(1)}, f32[2,24,8,128]{3,2,1,0:T(8,128)S(1)}, u32[]{:S(2)}, u32[]{:S(2)}) collective-permute-start(f32[2,24,8,128]{3,2,1,0:T(8,128)S(1)} %get-tuple-element.128), channel_id=1, source_target_pairs={{0,64},{32,96},{64,128},{96,160},{128,192},{160,224},{192,0},{224,... | collective-permute-start | bytes 589832 | tf_op jit(solution)/shard_map/ppermute | solution.py:285
  193.7 10.6 %collective-permute-start.37 = (f32[2,24,8,128]{3,2,1,0:T(8,128)S(1)}, f32[2,24,8,128]{3,2,1,0:T(8,128)S(1)}, u32[]{:S(2)}, u32[]{:S(2)}) collective-permute-start(f32[2,24,8,128]{3,2,1,0:T(8,128)S(1)} %get-tuple-element.127), channel_id=1, source_target_pairs={{0,192},{32,224},{64,0},{96,32},{128,64},{160,96},{192,128},{224,1... | collective-permute-start | bytes 589832 | tf_op jit(solution)/shard_map/ppermute | solution.py:289
  197.4 12.8 %collective-permute-start.26 = (f32[2,24,8,128]{3,2,1,0:T(8,128)S(1)}, f32[2,24,8,128]{3,2,1,0:T(8,128)S(1)}, u32[]{:S(2)}, u32[]{:S(2)}) collective-permute-start(f32[2,24,8,128]{3,2,1,0:T(8,128)S(1)} %get-tuple-element.134), channel_id=1, source_target_pairs={{0,64},{32,96},{64,128},{96,160},{128,192},{160,224},{192,0},{224,... | collective-permute-start | bytes 589832 | tf_op jit(solution)/shard_map/ppermute | solution.py:285
  197.5 13.0 %collective-permute-start.27 = (f32[2,24,8,128]{3,2,1,0:T(8,128)S(1)}, f32[2,24,8,128]{3,2,1,0:T(8,128)S(1)}, u32[]{:S(2)}, u32[]{:S(2)}) collective-permute-start(f32[2,24,8,128]{3,2,1,0:T(8,128)S(1)} %get-tuple-element.133), channel_id=1, source_target_pairs={{0,192},{32,224},{64,0},{96,32},{128,64},{160,96},{192,128},{224,1... | collective-permute-start | bytes 589832 | tf_op jit(solution)/shard_map/ppermute | solution.py:289
  204.3 9.9 %collective-permute-start.38 = (f32[1,24,8,128]{3,2,1,0:T(8,128)S(1)}, f32[1,24,8,128]{3,2,1,0:T(8,128)S(1)}, u32[]{:S(2)}, u32[]{:S(2)}) collective-permute-start(f32[1,24,8,128]{3,2,1,0:T(8,128)S(1)} %get-tuple-element.93), channel_id=1, source_target_pairs={{0,64},{32,96},{64,128},{96,160},{128,192},{160,224},{192,0},{224,... | collective-permute-start | bytes 294920 | tf_op jit(solution)/shard_map/ppermute | solution.py:285
  206.7 7.5 %collective-permute-start.39 = (f32[1,24,8,128]{3,2,1,0:T(8,128)S(1)}, f32[1,24,8,128]{3,2,1,0:T(8,128)S(1)}, u32[]{:S(2)}, u32[]{:S(2)}) collective-permute-start(f32[1,24,8,128]{3,2,1,0:T(8,128)S(1)} %get-tuple-element.94), channel_id=1, source_target_pairs={{0,192},{32,224},{64,0},{96,32},{128,64},{160,96},{192,128},{224,1... | collective-permute-start | bytes 294920 | tf_op jit(solution)/shard_map/ppermute | solution.py:289
  210.6 6.2 %collective-permute-start.28 = (f32[1,24,8,128]{3,2,1,0:T(8,128)S(1)}, f32[1,24,8,128]{3,2,1,0:T(8,128)S(1)}, u32[]{:S(2)}, u32[]{:S(2)}) collective-permute-start(f32[1,24,8,128]{3,2,1,0:T(8,128)S(1)} %get-tuple-element.83), channel_id=1, source_target_pairs={{0,64},{32,96},{64,128},{96,160},{128,192},{160,224},{192,0},{224,... | collective-permute-start | bytes 294920 | tf_op jit(solution)/shard_map/ppermute | solution.py:285
  212.2 4.6 %collective-permute-start.29 = (f32[1,24,8,128]{3,2,1,0:T(8,128)S(1)}, f32[1,24,8,128]{3,2,1,0:T(8,128)S(1)}, u32[]{:S(2)}, u32[]{:S(2)}) collective-permute-start(f32[1,24,8,128]{3,2,1,0:T(8,128)S(1)} %get-tuple-element.84), channel_id=1, source_target_pairs={{0,192},{32,224},{64,0},{96,32},{128,64},{160,96},{192,128},{224,1... | collective-permute-start | bytes 294920 | tf_op jit(solution)/shard_map/ppermute | solution.py:289
  217.0 17.5 %collective-permute-start.30 = (f32[2,24,8,128]{3,2,1,0:T(8,128)S(1)}, f32[2,24,8,128]{3,2,1,0:T(8,128)S(1)}, u32[]{:S(2)}, u32[]{:S(2)}) collective-permute-start(f32[2,24,8,128]{3,2,1,0:T(8,128)S(1)} %get-tuple-element.150), channel_id=1, source_target_pairs={{0,64},{32,96},{64,128},{96,160},{128,192},{160,224},{192,0},{224,... | collective-permute-start | bytes 589832 | tf_op jit(solution)/shard_map/ppermute | solution.py:285
  229.8 6.7 %collective-permute-start.31 = (f32[2,24,8,128]{3,2,1,0:T(8,128)S(1)}, f32[2,24,8,128]{3,2,1,0:T(8,128)S(1)}, u32[]{:S(2)}, u32[]{:S(2)}) collective-permute-start(f32[2,24,8,128]{3,2,1,0:T(8,128)S(1)} %get-tuple-element.150), channel_id=1, source_target_pairs={{0,192},{32,224},{64,0},{96,32},{128,64},{160,96},{192,128},{224,1... | collective-permute-start | bytes 589832 | tf_op jit(solution)/shard_map/ppermute | solution.py:289
  229.8 9.2 %collective-permute-start.40 = (f32[2,24,8,128]{3,2,1,0:T(8,128)S(1)}, f32[2,24,8,128]{3,2,1,0:T(8,128)S(1)}, u32[]{:S(2)}, u32[]{:S(2)}) collective-permute-start(f32[2,24,8,128]{3,2,1,0:T(8,128)S(1)} %get-tuple-element.149), channel_id=1, source_target_pairs={{0,64},{32,96},{64,128},{96,160},{128,192},{160,224},{192,0},{224,... | collective-permute-start | bytes 589832 | tf_op jit(solution)/shard_map/ppermute | solution.py:285
  232.2 10.5 %collective-permute-start.41 = (f32[2,24,8,128]{3,2,1,0:T(8,128)S(1)}, f32[2,24,8,128]{3,2,1,0:T(8,128)S(1)}, u32[]{:S(2)}, u32[]{:S(2)}) collective-permute-start(f32[2,24,8,128]{3,2,1,0:T(8,128)S(1)} %get-tuple-element.149), channel_id=1, source_target_pairs={{0,192},{32,224},{64,0},{96,32},{128,64},{160,96},{192,128},{224,1... | collective-permute-start | bytes 589832 | tf_op jit(solution)/shard_map/ppermute | solution.py:289
  236.6 8.9 %collective-permute-start.32 = (f32[1,24,8,128]{3,2,1,0:T(8,128)S(1)}, f32[1,24,8,128]{3,2,1,0:T(8,128)S(1)}, u32[]{:S(2)}, u32[]{:S(2)}) collective-permute-start(f32[1,24,8,128]{3,2,1,0:T(8,128)S(1)} %slice.385), channel_id=1, source_target_pairs={{0,64},{32,96},{64,128},{96,160},{128,192},{160,224},{192,0},{224,... | collective-permute-start | bytes 294920 | tf_op jit(solution)/shard_map/ppermute | solution.py:285
  242.7 5.7 %collective-permute-start.42 = (f32[1,24,8,128]{3,2,1,0:T(8,128)S(1)}, f32[1,24,8,128]{3,2,1,0:T(8,128)S(1)}, u32[]{:S(2)}, u32[]{:S(2)}) collective-permute-start(f32[1,24,8,128]{3,2,1,0:T(8,128)S(1)} %slice.400), channel_id=1, source_target_pairs={{0,64},{32,96},{64,128},{96,160},{128,192},{160,224},{192,0},{224,... | collective-permute-start | bytes 294920 | tf_op jit(solution)/shard_map/ppermute | solution.py:285
  245.5 4.7 %collective-permute-start.33 = (f32[1,24,8,128]{3,2,1,0:T(8,128)S(1)}, f32[1,24,8,128]{3,2,1,0:T(8,128)S(1)}, u32[]{:S(2)}, u32[]{:S(2)}) collective-permute-start(f32[1,24,8,128]{3,2,1,0:T(8,128)S(1)} %get-tuple-element.167), channel_id=1, source_target_pairs={{0,192},{32,224},{64,0},{96,32},{128,64},{160,96},{192,128},{224,1... | collective-permute-start | bytes 294920 | tf_op jit(solution)/shard_map/ppermute | solution.py:289
  248.4 5.0 %collective-permute-start.43 = (f32[1,24,8,128]{3,2,1,0:T(8,128)S(1)}, f32[1,24,8,128]{3,2,1,0:T(8,128)S(1)}, u32[]{:S(2)}, u32[]{:S(2)}) collective-permute-start(f32[1,24,8,128]{3,2,1,0:T(8,128)S(1)} %get-tuple-element.165), channel_id=1, source_target_pairs={{0,192},{32,224},{64,0},{96,32},{128,64},{160,96},{192,128},{224,1... | collective-permute-start | bytes 294920 | tf_op jit(solution)/shard_map/ppermute | solution.py:289
  250.3 6.8 %collective-permute-start.34 = (f32[8,24,8,128]{3,2,1,0:T(8,128)S(1)}, f32[8,24,8,128]{3,2,1,0:T(8,128)S(1)}, u32[]{:S(2)}, u32[]{:S(2)}) collective-permute-start(f32[8,24,8,128]{3,2,1,0:T(8,128)S(1)} %constant_dynamic-update-slice_fusion.4.refs_1_), channel_id=1, source_target_pairs={{0,32},{32,0},{64,96},{96,64},{128,160},{160,128},{192,224},{224,1... | collective-permute-start | bytes 2359304 | tf_op jit(solution)/shard_map/ppermute | solution.py:281
  253.6 5.4 %collective-permute-start.44 = (f32[8,24,8,128]{3,2,1,0:T(8,128)S(1)}, f32[8,24,8,128]{3,2,1,0:T(8,128)S(1)}, u32[]{:S(2)}, u32[]{:S(2)}) collective-permute-start(f32[8,24,8,128]{3,2,1,0:T(8,128)S(1)} %constant_dynamic-update-slice_fusion.9.refs_3_), channel_id=1, source_target_pairs={{0,32},{32,0},{64,96},{96,64},{128,160},{160,128},{192,224},{224,1... | collective-permute-start | bytes 2359304 | tf_op jit(solution)/shard_map/ppermute | solution.py:281
  (19 other events, 239.3 us)
where the time goes:
time: 262 us
  starting transfers between devices  121 us (46%)
  waiting for transfers between devices  99.8 us (38%)
  Pallas kernels  30.6 us (12%)
  local copies, waits for them, and re-layouts  6.21 us (2%)
  other arithmetic  3.17 us (1%)
    ppermute x12, waiting for transfers between devices, to_next(): return lax.ppermute(x, 'view', [(i, (i + 2) % 8) for i in range(8)])  38.7 us
    ppermute x5, starting transfers between devices, down(): return lax.ppermute(x, 'gz', [(i + 1, i) for i in range(n - 1)])  34.5 us
    ppermute x5, waiting for transfers between devices, up(): return lax.ppermute(x, 'gz', [(i, i + 1) for i in range(n - 1)])  34.3 us
    ppermute x12, starting transfers between devices, to_next(): return lax.ppermute(x, 'view', [(i, (i + 2) % 8) for i in range(8)])  29.3 us
    ppermute x11, starting transfers between devices, to_core(): return lax.ppermute(x, 'view', [(i, i ^ 1) for i in range(8)])  23.3 us
    ppermute x12, starting transfers between devices, to_prev(): return lax.ppermute(x, 'view', [(i, (i - 2) % 8) for i in range(8)])  23 us
    ppermute x12, waiting for transfers between devices, to_prev(): return lax.ppermute(x, 'view', [(i, (i - 2) % 8) for i in range(8)])  17.3 us
    pallas_call x2, Pallas kernels, middle(): pl.pallas_call(middle_kernel, out_shape=[half] * (2 * lots), in_specs=[pl...  14.3 us
  transfers between devices with their start and end apart: 45, of which 25 were waited for; matrix products, arithmetic and copies ran while one was open for 1% of the time, Pallas kernels for 4%

commit v1 on v0

--- a/solution.py
+++ b/solution.py
@@ -55,7 +55,7 @@
     return jnp.concatenate(blocks, 0) if len(blocks) > 1 else blocks[0]
 
 
-def lateral_kernel(counts, *refs):
+def lateral_kernel(counts, step, *refs):
     total = sum(c for c, _ in counts)
     ins, (left_ref, right_ref), outs = refs[:total], refs[total : total + 2], refs[total + 2 :]
     left = left_ref[...]
@@ -65,15 +65,15 @@
         region = ins[at : at + count]
         at += count
 
-        @pl.loop(0, planes // STEP)
+        @pl.loop(0, planes // step)
         def _(i, region=region, out=out):
-            zs = [STEP * i + j for j in range(STEP)]
+            zs = [step * i + j for j in range(step)]
             res = two_sided([region_plane(region, z) for z in zs], left, right)
             for j, z in enumerate(zs):
                 out[pl.ds(z * PITCH, N), :] = res[j * N : j * N + N]
 
 
-def lateral(regions, left, right):
+def lateral(regions, left, right, step=STEP):
     counts = []
     ins = []
     for region in regions:
@@ -82,7 +82,7 @@
         ins.extend(region)
     planes = sum(p for _, p in counts)
     return pl.pallas_call(
-        lambda *refs: lateral_kernel(counts, *refs),
+        lambda *refs: lateral_kernel(counts, step, *refs),
         out_shape=[jax.ShapeDtypeStruct((p * PITCH, N), F32) for _, p in counts],
         in_specs=[pl.BlockSpec(memory_space=pltpu.VMEM)] * (len(ins) + 2),
         out_specs=[pl.BlockSpec(memory_space=pltpu.VMEM)] * len(counts),
@@ -299,6 +299,11 @@
     return lax.ppermute(x, "gz", [(i + 1, i) for i in range(n - 1)])
 
 
+def cycle(x, step):
+    n = lax.axis_size("gz")
+    return lax.ppermute(x, "gz", [(i, (i + step) % n) for i in range(n)])
+
+
 def reduce_chunk(other, own):
     total = own + to_core(other)
     from_prev = to_next(total[0:2])
@@ -327,14 +332,20 @@
     order = jnp.stack([2 * opp, 2 * nxt + 1, 2 * opp + 1, 2 * prv, 2 * nxt, 2 * prv + 1, 2 * chip, 2 * chip + 1])
     starts = jnp.concatenate([core * 64 + 8 * order, (1 - core) * 64 + 8 * order, core[None]]).astype(jnp.int32)
 
-    before = up(lax.dynamic_slice(estimate, (SLAB - FAR, core * 64, 0), (FAR, 64, N)))
-    after = down(lax.dynamic_slice(estimate, (0, core * 64, 0), (FAR, 64, N)))
+    before = cycle(lax.dynamic_slice(estimate, (SLAB - FAR, core * 64, 0), (FAR, 64, N)), 1)
+    after = cycle(lax.dynamic_slice(estimate, (0, core * 64, 0), (FAR, 64, N)), -1)
     tf, ta, x_all, x_halves, x_fwd, adj_x, fwd_y, adj_y, rec_own, rec_first, rec_last = prep(
         starts, depth_taps, mx, my, recorded
     )
     before, after, rec_first, rec_last = lax.optimization_barrier((before, after, rec_first, rec_last))
-    rec_before = up(rec_last)
-    rec_after = down(rec_first)
+    slab = lax.axis_index("gz")
+
+    def clip(before, after):
+        there = slab > 0, slab < lax.axis_size("gz") - 1
+        return jnp.where(there[0], before, 0.0), jnp.where(there[1], after, 0.0)
+
+    rec_before, rec_after = cycle(rec_last, 1), cycle(rec_first, -1)
+    before, after = clip(before, after)
     before2, after2 = to_core(before), to_core(after)
 
     def log_sums(update, smooth):
@@ -345,8 +356,10 @@
     mine = lax.dynamic_slice(estimate, (0, core * 64 + chip * 16, 0), (SLAB, 16, N))
     mine = jnp.stack([mine[:, :8], mine[:, 8:]], 0)
 
-    (smooth_own,) = lateral([[estimate]], x_all, fwd_y)
-    smooth_b, smooth_a = lateral([[before, before2], [after, after2]], x_halves, fwd_y)
+    (smooth_own,) = lateral([[estimate]], x_all, fwd_y, 8)
+    smooth_b, smooth_a = lateral([[before, before2], [after, after2]], x_halves, fwd_y, 8)
+    rec_before, rec_after, smooth_b, smooth_a = lax.optimization_barrier((rec_before, rec_after, smooth_b, smooth_a))
+    rec_before, rec_after = clip(rec_before, rec_after)
     (log_sum,) = log_sums(0, (smooth_b, smooth_own, smooth_a))
     mine = mine * jnp.exp(log_sum / 8.0)
 
@@ -378,15 +391,14 @@
         x_fwd,
         fwd_y,
     )
-    lots = []
-    for k, log_sum in enumerate(log_sums(1, (smooth_b, smooth_own, smooth_a))):
-        planes = log_sum.shape[1]
-        chunk = mine[:, k * planes : (k + 1) * planes] * jnp.exp(log_sum / 8.0)
-        prev_c, next_c = lax.optimization_barrier((to_next(chunk), to_prev(chunk)))
-        opp_a, opp_b = to_next(prev_c[0:1]), to_prev(next_c[1:2])
-        ours = jnp.concatenate([opp_a, next_c[1:2], opp_b, prev_c[0:1], next_c[0:1], prev_c[1:2], chunk], 0)
-        lots.append([ours, to_core(ours)])
-    return place(starts, lots)
+    log_sum = jnp.concatenate(log_sums(1, (smooth_b, smooth_own, smooth_a)), 1)
+    mine = mine * jnp.exp(log_sum / 8.0)
+    prev_c, next_c = lax.optimization_barrier((to_next(mine), to_prev(mine)))
+    near = jnp.concatenate([mine, prev_c, next_c], 0)
+    near2 = to_core(near)
+    opp_c = jnp.concatenate([to_next(prev_c[0:1]), to_prev(next_c[1:2])], 0)
+    opp2 = to_core(opp_c)
+    return place(starts, [in_order(near, opp_c) + in_order(near2, opp2)])
 
 
 def solution(mesh):

time: 262 us -> 263 us (level)
  starting transfers between devices: 121 us -> 94.6 us
  waiting for transfers between devices: 99.8 us -> 125 us
  other arithmetic: 3.17 us -> 6.23 us
    ppermute x0 -> x4, waiting for transfers between devices: none -> 36.2 us  [cycle(): return lax.ppermute(x, 'gz', [(i, (i + step) % n) for i in range(n)])]
    ppermute x5 -> x3, waiting for transfers between devices: 34.3 us -> 6.63 us  [up(): return lax.ppermute(x, 'gz', [(i, i + 1) for i in range(n - 1)])]
    ppermute x12 -> x10, starting transfers between devices: 29.3 us -> 11.7 us  [to_next(): return lax.ppermute(x, 'view', [(i, (i + 2) % 8) for i in range(8)])]
    ppermute x5 -> x3, starting transfers between devices: 34.5 us -> 17.1 us  [down(): return lax.ppermute(x, 'gz', [(i + 1, i) for i in range(n - 1)])]
    ppermute x12 -> x10, waiting for transfers between devices: 38.7 us -> 54.9 us  [to_next(): return lax.ppermute(x, 'view', [(i, (i + 2) % 8) for i in range(8)])]
    ppermute x0 -> x4, starting transfers between devices: none -> 11.5 us  [cycle(): return lax.ppermute(x, 'gz', [(i, (i + step) % n) for i in range(n)])]
    ppermute x5 -> x3, starting transfers between devices: 10.8 us -> 5.76 us  [up(): return lax.ppermute(x, 'gz', [(i, i + 1) for i in range(n - 1)])]
    select_n x0 -> x3, other arithmetic: none -> 2.94 us  [clip(): return (jnp.where(there[0], before, 0.0), jnp.where(there[1], after, 0.0))]
  transfers between devices with their start and end apart: 45 -> 41, of which waited for: 25 -> 20; matrix products, arithmetic and copies ran while one was open for 1% -> 1% of each run, Pallas kernels for 4% -> 4%
where the time goes in v1:
time: 263 us
  waiting for transfers between devices  125 us (48%)
  starting transfers between devices  94.6 us (36%)
  Pallas kernels  31.5 us (12%)
  other arithmetic  6.23 us (2%)
  local copies, waits for them, and re-layouts  4.46 us (2%)
    ppermute x10, waiting for transfers between devices, to_next(): return lax.ppermute(x, 'view', [(i, (i + 2) % 8) for i in range(8)])  54.9 us
    ppermute x4, waiting for transfers between devices, cycle(): return lax.ppermute(x, 'gz', [(i, (i + step) % n) for i in range(n)])  36.2 us
    ppermute x10, starting transfers between devices, to_prev(): return lax.ppermute(x, 'view', [(i, (i - 2) % 8) for i in range(8)])  25.6 us
    ppermute x11, starting transfers between devices, to_core(): return lax.ppermute(x, 'view', [(i, i ^ 1) for i in range(8)])  23 us
    ppermute x10, waiting for transfers between devices, to_prev(): return lax.ppermute(x, 'view', [(i, (i - 2) % 8) for i in range(8)])  20 us
    ppermute x3, starting transfers between devices, down(): return lax.ppermute(x, 'gz', [(i + 1, i) for i in range(n - 1)])  17.1 us
    pallas_call x2, Pallas kernels, middle(): pl.pallas_call(middle_kernel, out_shape=[half] * (2 * lots), in_specs=[pl...  14.4 us
    pallas_call x4, Pallas kernels, lateral(): pl.pallas_call(lambda *refs: lateral_kernel(counts, step, *refs), out_sha...  12.9 us
  transfers between devices with their start and end apart: 41, of which 20 were waited for; matrix products, arithmetic and copies ran while one was open for 1% of the time, Pallas kernels for 4%

profile of v1, /device:TPU:33, one launch (start us, length us, event | category | flops | bytes accessed | tf_op | source)
XLA Modules:
  0.0 262.7 jit_solution(9921239499257284453)
XLA Ops:
  0.0 3.3 %constant_dynamic-slice_fusion = (f32[32,64,128]{2,1,0:T(8,128)}, f32[32,64,128]{2,1,0:T(8,128)}) fusion(f32[48,128,128]{2,1,0:T(8,128)} %refs_0_.1, s32[]{:T(128)S(6)} %select_n.54), kind=kLoop, calls=%fused_computation.39 | loop fusion | bytes 4194308 | tf_op jit(solution)/shard_map/dynamic_slice | solution.py:336
  4.5 4.5 %collective-permute-start.1 = (f32[32,64,128]{2,1,0:T(8,128)}, f32[32,64,128]{2,1,0:T(8,128)}, u32[]{:S(2)}, u32[]{:S(2)}) collective-permute-start(f32[32,64,128]{2,1,0:T(8,128)} %get-tuple-element.103), channel_id=1, source_target_pairs={{0,31},{1,0},{2,1},{3,2},{4,3},{5,4},{6,5},{7,6},{8,7},{9,8},{10,9... | collective-permute-start | bytes 3145736 | tf_op jit(solution)/shard_map/ppermute | solution.py:304
  9.2 1.7 prep.1
  10.9 20.9 %collective-permute-done = f32[32,64,128]{2,1,0:T(8,128)} collective-permute-done((f32[32,64,128]{2,1,0:T(8,128)}, f32[32,64,128]{2,1,0:T(8,128)}, u32[]{:S(2)}, u32[]{:S(2)}) %collective-permute-start) | collective-permute-done | bytes 1048608 | tf_op jit(solution)/shard_map/ppermute | solution.py:304
  36.5 5.8 %collective-permute-start.3 = (f32[128,16,128]{2,1,0:T(8,128)S(1)}, f32[128,16,128]{2,1,0:T(8,128)S(1)}, u32[]{:S(2)}, u32[]{:S(2)}) collective-permute-start(f32[128,16,128]{2,1,0:T(8,128)S(1)} %get-tuple-element.57), channel_id=1, source_target_pairs={{0,31},{1,0},{2,1},{3,2},{4,3},{5,4},{6,5},{7,6},{8,7},{9,8},{10,9... | collective-permute-start | bytes 3145736 | tf_op jit(solution)/shard_map/ppermute | solution.py:304
  42.3 3.2 %lateral.5.so = f32[6336,128]{1,0:T(8,128)S(1)} custom-call(f32[48,128,128]{2,1,0:T(8,128)S(1)} %copy-done, bf16[256,256]{1,0:T(8,128)(2,1)S(1)} %get-tuple-element.65.refs_1_, bf16[256,256]{1,0:T(8,128)(2,1)S(1)} %get-tuple-element.61.refs_5_.refs_2_.refs_29_.refs_15_), custom_call_target="tpu_custom_call" | custom-call | flops 1610612736 | bytes 6291456 | tf_op jit(solution)/shard_map/lateral/pallas_call | solution.py:84
  45.5 4.3 %lateral.4 = (f32[4224,128]{1,0:T(8,128)S(1)}, f32[4224,128]{1,0:T(8,128)S(1)}) custom-call(f32[32,64,128]{2,1,0:T(8,128)S(1)} %broadcast_select_fusion.3.refs_0_, f32[32,64,128]{2,1,0:T(8,128)S(1)} %collective-permute-done.4.refs_1_, f32[32,64,128]{2,1,0:T(8,128)S(1)} %broadcast_select_fusion.2.refs_2_, f32[32,64,128]{2,1,0:T(8,128)S(1)} %collective-permute-done.5.refs_3_, ...), custom_call_target="tpu_custom_call" | custom-call | flops 2147483648 | bytes 8388608 | tf_op jit(solution)/shard_map/lateral/pallas_call | solution.py:84
  49.8 15.2 %collective-permute-done.2 = f32[128,16,128]{2,1,0:T(8,128)S(1)} collective-permute-done((f32[128,16,128]{2,1,0:T(8,128)S(1)}, f32[128,16,128]{2,1,0:T(8,128)S(1)}, u32[]{:S(2)}, u32[]{:S(2)}) %collective-permute-start.2) | collective-permute-done | bytes 1048608 | tf_op jit(solution)/shard_map/ppermute | solution.py:304
  65.2 6.7 %middle.2 = (f32[8,48,8,128]{3,2,1,0:T(8,128)S(1)}, f32[8,48,8,128]{3,2,1,0:T(8,128)S(1)}) custom-call(f32[4224,128]{1,0:T(8,128)S(1)} %get-tuple-element.64.sb, f32[6336,128]{1,0:T(8,128)S(1)} %lateral.5.so, f32[4224,128]{1,0:T(8,128)S(1)} %get-tuple-element.66.sa, f32[128,16,128]{2,1,0:T(8,128)S(1)} %get-tuple-element.180.mb, ...), custom_call_target="tpu_custom_call" | custom-call | flops 8000000000 | bytes 15728640 | tf_op jit(solution)/shard_map/middle/pallas_call | solution.py:156
  73.3 3.0 %collective-permute-done.6 = f32[8,48,8,128]{3,2,1,0:T(8,128)S(1)} collective-permute-done((f32[8,48,8,128]{3,2,1,0:T(8,128)S(1)}, f32[8,48,8,128]{3,2,1,0:T(8,128)S(1)}, u32[]{:S(2)}, u32[]{:S(2)}) %collective-permute-start.6) | collective-permute-done | bytes 1572896 | tf_op jit(solution)/shard_map/ppermute | solution.py:281
  76.6 3.1 %collective-permute-start.7 = (f32[2,48,8,128]{3,2,1,0:T(8,128)S(1)}, f32[2,48,8,128]{3,2,1,0:T(8,128)S(1)}, u32[]{:S(2)}, u32[]{:S(2)}) collective-permute-start(f32[2,48,8,128]{3,2,1,0:T(8,128)S(1)} %get-tuple-element.122), channel_id=1, source_target_pairs={{0,64},{32,96},{64,128},{96,160},{128,192},{160,224},{192,0},{224,... | collective-permute-start | bytes 1179656 | tf_op jit(solution)/shard_map/ppermute | solution.py:285
  79.7 2.2 collective-permute-start.8
  81.9 17.2 %collective-permute-done.7 = f32[2,48,8,128]{3,2,1,0:T(8,128)S(1)} collective-permute-done((f32[2,48,8,128]{3,2,1,0:T(8,128)S(1)}, f32[2,48,8,128]{3,2,1,0:T(8,128)S(1)}, u32[]{:S(2)}, u32[]{:S(2)}) %collective-permute-start.7) | collective-permute-done | bytes 393248 | tf_op jit(solution)/shard_map/ppermute | solution.py:285
  101.1 2.5 collective-permute-start.9
  104.7 4.0 %collective-permute-done.9 = f32[1,48,8,128]{3,2,1,0:T(8,128)} collective-permute-done((f32[1,48,8,128]{3,2,1,0:T(8,128)}, f32[1,48,8,128]{3,2,1,0:T(8,128)}, u32[]{:S(2)}, u32[]{:S(2)}) %collective-permute-start.9) | collective-permute-done | bytes 196640 | tf_op jit(solution)/shard_map/ppermute | solution.py:285
  108.7 4.4 %collective-permute-done.10 = f32[1,48,8,128]{3,2,1,0:T(8,128)} collective-permute-done((f32[1,48,8,128]{3,2,1,0:T(8,128)}, f32[1,48,8,128]{3,2,1,0:T(8,128)}, u32[]{:S(2)}, u32[]{:S(2)}) %collective-permute-start.10) | collective-permute-done | bytes 196640 | tf_op jit(solution)/shard_map/ppermute | solution.py:289
  115.1 3.3 %collective-permute-start.13 = (f32[2,48,8,128]{3,2,1,0:T(8,128)S(1)}, f32[2,48,8,128]{3,2,1,0:T(8,128)S(1)}, u32[]{:S(2)}, u32[]{:S(2)}) collective-permute-start(f32[2,48,8,128]{3,2,1,0:T(8,128)S(1)} %maximum_multiply_fusion.refs_6_), channel_id=1, source_target_pairs={{0,192},{32,224},{64,0},{96,32},{128,64},{160,96},{192,128},{224,1... | collective-permute-start | bytes 1179656 | tf_op jit(solution)/shard_map/ppermute | solution.py:289
  118.4 9.0 %collective-permute-done.11 = f32[2,48,8,128]{3,2,1,0:T(8,128)S(1)} collective-permute-done((f32[2,48,8,128]{3,2,1,0:T(8,128)S(1)}, f32[2,48,8,128]{3,2,1,0:T(8,128)S(1)}, u32[]{:S(2)}, u32[]{:S(2)}) %collective-permute-start.11) | collective-permute-done | bytes 393248 | tf_op jit(solution)/shard_map/ppermute | solution.py:285
  127.5 2.5 collective-permute-done.13
  130.0 4.4 %collective-permute-start.14 = (f32[1,48,8,128]{3,2,1,0:T(8,128)S(1)}, f32[1,48,8,128]{3,2,1,0:T(8,128)S(1)}, u32[]{:S(2)}, u32[]{:S(2)}) collective-permute-start(f32[1,48,8,128]{3,2,1,0:T(8,128)S(1)} %get-tuple-element.168.refs_1_), channel_id=1, source_target_pairs={{0,192},{32,224},{64,0},{96,32},{128,64},{160,96},{192,128},{224,1... | collective-permute-start | bytes 589832 | tf_op jit(solution)/shard_map/ppermute | solution.py:289
  134.6 1.9 collective-permute-start.16
  136.5 7.6 %collective-permute-start.21 = (f32[4,32,8,128]{3,2,1,0:T(8,128)S(1)}, f32[4,32,8,128]{3,2,1,0:T(8,128)S(1)}, u32[]{:S(2)}, u32[]{:S(2)}) collective-permute-start(f32[4,32,8,128]{3,2,1,0:T(8,128)S(1)} %get-tuple-element.143), channel_id=1, source_target_pairs={{1,0},{2,1},{3,2},{4,3},{5,4},{6,5},{7,6},{8,7},{9,8},{10,9},{11,1... | collective-permute-start | bytes 1572872 | tf_op jit(solution)/shard_map/ppermute | solution.py:299
  144.2 1.9 collective-permute-start.15
  146.1 7.6 %collective-permute-start.18 = (f32[2,32,8,128]{3,2,1,0:T(8,128)S(1)}, f32[2,32,8,128]{3,2,1,0:T(8,128)S(1)}, u32[]{:S(2)}, u32[]{:S(2)}) collective-permute-start(f32[2,32,8,128]{3,2,1,0:T(8,128)S(1)} %get-tuple-element.171), channel_id=1, source_target_pairs={{1,0},{2,1},{3,2},{4,3},{5,4},{6,5},{7,6},{8,7},{9,8},{10,9},{11,1... | collective-permute-start | bytes 786440 | tf_op jit(solution)/shard_map/ppermute | solution.py:299
  153.7 1.9 collective-permute-start.17
  155.8 6.6 %collective-permute-done.15 = f32[2,32,8,128]{3,2,1,0:T(8,128)S(1)} collective-permute-done((f32[2,32,8,128]{3,2,1,0:T(8,128)S(1)}, f32[2,32,8,128]{3,2,1,0:T(8,128)S(1)}, u32[]{:S(2)}, u32[]{:S(2)}) %collective-permute-start.15) | collective-permute-done | bytes 262176 | tf_op jit(solution)/shard_map/ppermute | solution.py:294
  162.4 1.9 collective-permute-start.20
  164.3 7.6 %collective-permute-start.24 = (f32[6,48,8,128]{3,2,1,0:T(8,128)S(1)}, f32[6,48,8,128]{3,2,1,0:T(8,128)S(1)}, u32[]{:S(2)}, u32[]{:S(2)}) collective-permute-start(f32[6,48,8,128]{3,2,1,0:T(8,128)S(1)} %pad_maximum_fusion.1), channel_id=1, source_target_pairs={{0,32},{32,0},{64,96},{96,64},{128,160},{160,128},{192,224},{224,1... | collective-permute-start | bytes 3538952 | tf_op jit(solution)/shard_map/ppermute | solution.py:281
  171.9 2.1 collective-permute-start.23
  174.1 1.8 collective-permute-start.19
  177.6 2.3 lateral.7.so
  180.1 3.1 %lateral.6 = (f32[4224,128]{1,0:T(8,128)S(1)}, f32[4224,128]{1,0:T(8,128)S(1)}) custom-call(f32[1,32,8,128]{3,2,1,0:T(8,128)S(1)} %get-tuple-element.176.refs_0_, f32[1,32,8,128]{3,2,1,0:T(8,128)S(1)} %get-tuple-element.156.refs_1_, f32[1,32,8,128]{3,2,1,0:T(8,128)S(1)} %get-tuple-element.175.refs_2_, f32[1,32,8,128]{3,2,1,0:T(8,128)S(1)} %get-tuple-element.155.refs_3_, ...), custom_call_target="tpu_custom_call" | custom-call | flops 2147483648 | bytes 8388608 | tf_op jit(solution)/shard_map/lateral/pallas_call | solution.py:84
  183.2 7.6 %middle.3 = (f32[8,24,8,128]{3,2,1,0:T(8,128)S(1)}, f32[8,24,8,128]{3,2,1,0:T(8,128)S(1)}, f32[8,24,8,128]{3,2,1,0:T(8,128)S(1)}, f32[8,24,8,128]{3,2,1,0:T(8,128)S(1)}) custom-call(f32[4224,128]{1,0:T(8,128)S(1)} %get-tuple-element.83.sb, f32[6336,128]{1,0:T(8,128)S(1)} %lateral.7.so, f32[4224,128]{1,0:T(8,128)S(1)} %get-tuple-element.84.sa, ...), custom_call_target="tpu_custom_call" | custom-call | flops 8000000000 | bytes 15728640 | tf_op jit(solution)/shard_map/middle/pallas_call | solution.py:156
  191.5 1.8 collective-permute-done.30
  193.4 3.6 %collective-permute-start.32 = (f32[2,24,8,128]{3,2,1,0:T(8,128)S(1)}, f32[2,24,8,128]{3,2,1,0:T(8,128)S(1)}, u32[]{:S(2)}, u32[]{:S(2)}) collective-permute-start(f32[2,24,8,128]{3,2,1,0:T(8,128)S(1)} %get-tuple-element.141), channel_id=1, source_target_pairs={{0,192},{32,224},{64,0},{96,32},{128,64},{160,96},{192,128},{224,1... | collective-permute-start | bytes 589832 | tf_op jit(solution)/shard_map/ppermute | solution.py:289
  197.2 3.6 %collective-permute-start.27 = (f32[2,24,8,128]{3,2,1,0:T(8,128)S(1)}, f32[2,24,8,128]{3,2,1,0:T(8,128)S(1)}, u32[]{:S(2)}, u32[]{:S(2)}) collective-permute-start(f32[2,24,8,128]{3,2,1,0:T(8,128)S(1)} %get-tuple-element.135), channel_id=1, source_target_pairs={{0,192},{32,224},{64,0},{96,32},{128,64},{160,96},{192,128},{224,1... | collective-permute-start | bytes 589832 | tf_op jit(solution)/shard_map/ppermute | solution.py:289
  200.8 6.3 %collective-permute-done.31 = f32[2,24,8,128]{3,2,1,0:T(8,128)S(1)} collective-permute-done((f32[2,24,8,128]{3,2,1,0:T(8,128)S(1)}, f32[2,24,8,128]{3,2,1,0:T(8,128)S(1)}, u32[]{:S(2)}, u32[]{:S(2)}) %collective-permute-start.31) | collective-permute-done | bytes 196640 | tf_op jit(solution)/shard_map/ppermute | solution.py:285
  207.1 2.3 collective-permute-done.32
  209.8 3.3 %collective-permute-start.34 = (f32[1,24,8,128]{3,2,1,0:T(8,128)S(1)}, f32[1,24,8,128]{3,2,1,0:T(8,128)S(1)}, u32[]{:S(2)}, u32[]{:S(2)}) collective-permute-start(f32[1,24,8,128]{3,2,1,0:T(8,128)S(1)} %get-tuple-element.98), channel_id=1, source_target_pairs={{0,192},{32,224},{64,0},{96,32},{128,64},{160,96},{192,128},{224,1... | collective-permute-start | bytes 294920 | tf_op jit(solution)/shard_map/ppermute | solution.py:289
  213.1 1.9 collective-permute-done.27
  215.4 3.3 %collective-permute-start.29 = (f32[1,24,8,128]{3,2,1,0:T(8,128)S(1)}, f32[1,24,8,128]{3,2,1,0:T(8,128)S(1)}, u32[]{:S(2)}, u32[]{:S(2)}) collective-permute-start(f32[1,24,8,128]{3,2,1,0:T(8,128)S(1)} %get-tuple-element.90), channel_id=1, source_target_pairs={{0,192},{32,224},{64,0},{96,32},{128,64},{160,96},{192,128},{224,1... | collective-permute-start | bytes 294920 | tf_op jit(solution)/shard_map/ppermute | solution.py:289
  219.2 6.8 %collective-permute-done.28 = f32[1,24,8,128]{3,2,1,0:T(8,128)S(1)} collective-permute-done((f32[1,24,8,128]{3,2,1,0:T(8,128)S(1)}, f32[1,24,8,128]{3,2,1,0:T(8,128)S(1)}, u32[]{:S(2)}, u32[]{:S(2)}) %collective-permute-start.28) | collective-permute-done | bytes 98336 | tf_op jit(solution)/shard_map/ppermute | solution.py:285
  226.2 2.9 %collective-permute-start.35 = (f32[2,48,8,128]{3,2,1,0:T(8,128)S(1)}, f32[2,48,8,128]{3,2,1,0:T(8,128)S(1)}, u32[]{:S(2)}, u32[]{:S(2)}) collective-permute-start(f32[2,48,8,128]{3,2,1,0:T(8,128)S(1)} %fusion.2.refs_7_), channel_id=1, source_target_pairs={{0,64},{32,96},{64,128},{96,160},{128,192},{160,224},{192,0},{224,... | collective-permute-start | bytes 1179656 | tf_op jit(solution)/shard_map/ppermute | solution.py:285
  229.8 11.6 %collective-permute-done.35 = f32[2,48,8,128]{3,2,1,0:T(8,128)S(1)} collective-permute-done((f32[2,48,8,128]{3,2,1,0:T(8,128)S(1)}, f32[2,48,8,128]{3,2,1,0:T(8,128)S(1)}, u32[]{:S(2)}, u32[]{:S(2)}) %collective-permute-start.35) | collective-permute-done | bytes 393248 | tf_op jit(solution)/shard_map/ppermute | solution.py:285
  241.4 1.7 collective-permute-start.37
  243.3 6.9 %collective-permute-start.40 = (f32[6,48,8,128]{3,2,1,0:T(8,128)S(1)}, f32[6,48,8,128]{3,2,1,0:T(8,128)S(1)}, u32[]{:S(2)}, u32[]{:S(2)}) collective-permute-start(f32[6,48,8,128]{3,2,1,0:T(8,128)S(1)} %pad_maximum_fusion.2), channel_id=1, source_target_pairs={{0,32},{32,0},{64,96},{96,64},{128,160},{160,128},{192,224},{224,1... | collective-permute-start | bytes 3538952 | tf_op jit(solution)/shard_map/ppermute | solution.py:281
  250.3 7.4 %collective-permute-done.38.refs_3_ = f32[1,48,8,128]{3,2,1,0:T(8,128)S(1)} collective-permute-done((f32[1,48,8,128]{3,2,1,0:T(8,128)S(1)}, f32[1,48,8,128]{3,2,1,0:T(8,128)S(1)}, u32[]{:S(2)}, u32[]{:S(2)}) %collective-permute-start.38) | collective-permute-done | bytes 196640 | tf_op jit(solution)/shard_map/ppermute | solution.py:289
  260.1 2.6 place.1
  (137 shorter events, 20.8 us)
Async XLA Ops:
  3.3 28.6 %collective-permute-start = (f32[32,64,128]{2,1,0:T(8,128)}, f32[32,64,128]{2,1,0:T(8,128)}, u32[]{:S(2)}, u32[]{:S(2)}) collective-permute-start(f32[32,64,128]{2,1,0:T(8,128)} %get-tuple-element.104), channel_id=1, source_target_pairs={{0,1},{1,2},{2,3},{3,4},{4,5},{5,6},{6,7},{7,8},{8,9},{9,10},{10,1... | collective-permute-start | bytes 3145736 | tf_op jit(solution)/shard_map/ppermute | solution.py:304
  4.5 27.4 %collective-permute-start.1 = (f32[32,64,128]{2,1,0:T(8,128)}, f32[32,64,128]{2,1,0:T(8,128)}, u32[]{:S(2)}, u32[]{:S(2)}) collective-permute-start(f32[32,64,128]{2,1,0:T(8,128)} %get-tuple-element.103), channel_id=1, source_target_pairs={{0,31},{1,0},{2,1},{3,2},{4,3},{5,4},{6,5},{7,6},{8,7},{9,8},{10,9... | collective-permute-start | bytes 3145736 | tf_op jit(solution)/shard_map/ppermute | solution.py:304
  10.9 54.3 %copy-start.9 = (f32[128,48,128]{2,1,0:T(8,128)}, f32[128,48,128]{2,1,0:T(8,128)S(1)}, u32[]{:S(2)}) copy-start(f32[128,48,128]{2,1,0:T(8,128)S(1)} %get-tuple-element.68.mo) | copy-start | bytes 9437188
  10.9 54.3 %copy-start.11 = (bf16[256,256]{1,0:T(8,128)(2,1)}, bf16[256,256]{1,0:T(8,128)(2,1)S(1)}, u32[]{:S(2)}) copy-start(bf16[256,256]{1,0:T(8,128)(2,1)S(1)} %get-tuple-element.72.left_ref) | copy-start | bytes 393220
  10.9 54.3 %copy-start.13 = (bf16[256,256]{1,0:T(8,128)(2,1)}, bf16[256,256]{1,0:T(8,128)(2,1)S(1)}, u32[]{:S(2)}) copy-start(bf16[256,256]{1,0:T(8,128)(2,1)S(1)} %get-tuple-element.73.right_ref) | copy-start | bytes 393220
  10.9 54.3 %copy-start.15 = (bf16[160,224]{1,0:T(8,128)(2,1)}, bf16[160,224]{1,0:T(8,128)(2,1)S(1)}, u32[]{:S(2)}) copy-start(bf16[160,224]{1,0:T(8,128)(2,1)S(1)} %get-tuple-element.70.tf_ref) | copy-start | bytes 215044
  10.9 54.3 %copy-start.17 = (bf16[96,160]{1,0:T(8,128)(2,1)}, bf16[96,160]{1,0:T(8,128)(2,1)S(1)}, u32[]{:S(2)}) copy-start(bf16[96,160]{1,0:T(8,128)(2,1)S(1)} %get-tuple-element.71.ta_ref) | copy-start | bytes 92164
  31.9 10.4 %copy-start = (f32[48,128,128]{2,1,0:T(8,128)S(1)}, f32[48,128,128]{2,1,0:T(8,128)}, u32[]{:S(2)}) copy-start(f32[48,128,128]{2,1,0:T(8,128)} %refs_0_.1) | copy-start | bytes 9437188
  33.3 12.1 %collective-permute-start.4 = (f32[32,64,128]{2,1,0:T(8,128)S(1)}, f32[32,64,128]{2,1,0:T(8,128)S(1)}, u32[]{:S(2)}, u32[]{:S(2)}) collective-permute-start(f32[32,64,128]{2,1,0:T(8,128)S(1)} %broadcast_select_fusion.3.refs_0_), channel_id=1, source_target_pairs={{0,32},{32,0},{64,96},{96,64},{128,160},{160,128},{192,224},{224,1... | collective-permute-start | bytes 3145736 | tf_op jit(solution)/shard_map/ppermute | solution.py:281
  36.3 9.2 %collective-permute-start.5 = (f32[32,64,128]{2,1,0:T(8,128)S(1)}, f32[32,64,128]{2,1,0:T(8,128)S(1)}, u32[]{:S(2)}, u32[]{:S(2)}) collective-permute-start(f32[32,64,128]{2,1,0:T(8,128)S(1)} %broadcast_select_fusion.2.refs_2_), channel_id=1, source_target_pairs={{0,32},{32,0},{64,96},{96,64},{128,160},{160,128},{192,224},{224,1... | collective-permute-start | bytes 3145736 | tf_op jit(solution)/shard_map/ppermute | solution.py:281
  36.4 28.6 %collective-permute-start.2 = (f32[128,16,128]{2,1,0:T(8,128)S(1)}, f32[128,16,128]{2,1,0:T(8,128)S(1)}, u32[]{:S(2)}, u32[]{:S(2)}) collective-permute-start(f32[128,16,128]{2,1,0:T(8,128)S(1)} %get-tuple-element.56), channel_id=1, source_target_pairs={{0,1},{1,2},{2,3},{3,4},{4,5},{5,6},{6,7},{7,8},{8,9},{9,10},{10,1... | collective-permute-start | bytes 3145736 | tf_op jit(solution)/shard_map/ppermute | solution.py:304
  36.5 28.5 %collective-permute-start.3 = (f32[128,16,128]{2,1,0:T(8,128)S(1)}, f32[128,16,128]{2,1,0:T(8,128)S(1)}, u32[]{:S(2)}, u32[]{:S(2)}) collective-permute-start(f32[128,16,128]{2,1,0:T(8,128)S(1)} %get-tuple-element.57), channel_id=1, source_target_pairs={{0,31},{1,0},{2,1},{3,2},{4,3},{5,4},{6,5},{7,6},{8,7},{9,8},{10,9... | collective-permute-start | bytes 3145736 | tf_op jit(solution)/shard_map/ppermute | solution.py:304
  72.0 4.4 %collective-permute-start.6 = (f32[8,48,8,128]{3,2,1,0:T(8,128)S(1)}, f32[8,48,8,128]{3,2,1,0:T(8,128)S(1)}, u32[]{:S(2)}, u32[]{:S(2)}) collective-permute-start(f32[8,48,8,128]{3,2,1,0:T(8,128)S(1)} %get-tuple-element.75), channel_id=1, source_target_pairs={{0,32},{32,0},{64,96},{96,64},{128,160},{160,128},{192,224},{224,1... | collective-permute-start | bytes 4718600 | tf_op jit(solution)/shard_map/ppermute | solution.py:281
  76.5 23.6 %copy-start.19 = (f32[8,48,8,128]{3,2,1,0:T(8,128)}, f32[8,48,8,128]{3,2,1,0:T(8,128)S(1)}, u32[]{:S(2)}) copy-start(f32[8,48,8,128]{3,2,1,0:T(8,128)S(1)} %add.133) | copy-start | bytes 4718596
  76.6 22.5 %collective-permute-start.7 = (f32[2,48,8,128]{3,2,1,0:T(8,128)S(1)}, f32[2,48,8,128]{3,2,1,0:T(8,128)S(1)}, u32[]{:S(2)}, u32[]{:S(2)}) collective-permute-start(f32[2,48,8,128]{3,2,1,0:T(8,128)S(1)} %get-tuple-element.122), channel_id=1, source_target_pairs={{0,64},{32,96},{64,128},{96,160},{128,192},{160,224},{192,0},{224,... | collective-permute-start | bytes 1179656 | tf_op jit(solution)/shard_map/ppermute | solution.py:285
  79.7 20.5 %collective-permute-start.8 = (f32[2,48,8,128]{3,2,1,0:T(8,128)S(1)}, f32[2,48,8,128]{3,2,1,0:T(8,128)S(1)}, u32[]{:S(2)}, u32[]{:S(2)}) collective-permute-start(f32[2,48,8,128]{3,2,1,0:T(8,128)S(1)} %get-tuple-element.121), channel_id=1, source_target_pairs={{0,192},{32,224},{64,0},{96,32},{128,64},{160,96},{192,128},{224,1... | collective-permute-start | bytes 1179656 | tf_op jit(solution)/shard_map/ppermute | solution.py:289
  101.1 7.6 %collective-permute-start.9 = (f32[1,48,8,128]{3,2,1,0:T(8,128)}, f32[1,48,8,128]{3,2,1,0:T(8,128)}, u32[]{:S(2)}, u32[]{:S(2)}) collective-permute-start(f32[1,48,8,128]{3,2,1,0:T(8,128)} %get-tuple-element.78), channel_id=1, source_target_pairs={{0,64},{32,96},{64,128},{96,160},{128,192},{160,224},{192,0},{224,... | collective-permute-start | bytes 589832 | tf_op jit(solution)/shard_map/ppermute | solution.py:285
  103.6 9.5 %collective-permute-start.10 = (f32[1,48,8,128]{3,2,1,0:T(8,128)}, f32[1,48,8,128]{3,2,1,0:T(8,128)}, u32[]{:S(2)}, u32[]{:S(2)}) collective-permute-start(f32[1,48,8,128]{3,2,1,0:T(8,128)} %get-tuple-element.79), channel_id=1, source_target_pairs={{0,192},{32,224},{64,0},{96,32},{128,64},{160,96},{192,128},{224,1... | collective-permute-start | bytes 589832 | tf_op jit(solution)/shard_map/ppermute | solution.py:289
  114.5 12.8 %collective-permute-start.11 = (f32[2,48,8,128]{3,2,1,0:T(8,128)S(1)}, f32[2,48,8,128]{3,2,1,0:T(8,128)S(1)}, u32[]{:S(2)}, u32[]{:S(2)}) collective-permute-start(f32[2,48,8,128]{3,2,1,0:T(8,128)S(1)} %maximum_multiply_fusion.refs_6_), channel_id=1, source_target_pairs={{0,64},{32,96},{64,128},{96,160},{128,192},{160,224},{192,0},{224,... | collective-permute-start | bytes 1179656 | tf_op jit(solution)/shard_map/ppermute | solution.py:285
  115.1 14.9 %collective-permute-start.13 = (f32[2,48,8,128]{3,2,1,0:T(8,128)S(1)}, f32[2,48,8,128]{3,2,1,0:T(8,128)S(1)}, u32[]{:S(2)}, u32[]{:S(2)}) collective-permute-start(f32[2,48,8,128]{3,2,1,0:T(8,128)S(1)} %maximum_multiply_fusion.refs_6_), channel_id=1, source_target_pairs={{0,192},{32,224},{64,0},{96,32},{128,64},{160,96},{192,128},{224,1... | collective-permute-start | bytes 1179656 | tf_op jit(solution)/shard_map/ppermute | solution.py:289
  127.4 16.7 %collective-permute-start.12 = (f32[1,48,8,128]{3,2,1,0:T(8,128)S(1)}, f32[1,48,8,128]{3,2,1,0:T(8,128)S(1)}, u32[]{:S(2)}, u32[]{:S(2)}) collective-permute-start(f32[1,48,8,128]{3,2,1,0:T(8,128)S(1)} %get-tuple-element.166.refs_3_), channel_id=1, source_target_pairs={{0,64},{32,96},{64,128},{96,160},{128,192},{160,224},{192,0},{224,... | collective-permute-start | bytes 589832 | tf_op jit(solution)/shard_map/ppermute | solution.py:285
  130.0 14.1 %collective-permute-start.14 = (f32[1,48,8,128]{3,2,1,0:T(8,128)S(1)}, f32[1,48,8,128]{3,2,1,0:T(8,128)S(1)}, u32[]{:S(2)}, u32[]{:S(2)}) collective-permute-start(f32[1,48,8,128]{3,2,1,0:T(8,128)S(1)} %get-tuple-element.168.refs_1_), channel_id=1, source_target_pairs={{0,192},{32,224},{64,0},{96,32},{128,64},{160,96},{192,128},{224,1... | collective-permute-start | bytes 589832 | tf_op jit(solution)/shard_map/ppermute | solution.py:289
  134.6 41.3 %collective-permute-start.16 = (f32[4,32,8,128]{3,2,1,0:T(8,128)S(1)}, f32[4,32,8,128]{3,2,1,0:T(8,128)S(1)}, u32[]{:S(2)}, u32[]{:S(2)}) collective-permute-start(f32[4,32,8,128]{3,2,1,0:T(8,128)S(1)} %get-tuple-element.144), channel_id=1, source_target_pairs={{0,1},{1,2},{2,3},{3,4},{4,5},{5,6},{6,7},{7,8},{8,9},{9,10},{10,1... | collective-permute-start | bytes 1572872 | tf_op jit(solution)/shard_map/ppermute | solution.py:294
  136.5 39.4 %collective-permute-start.21 = (f32[4,32,8,128]{3,2,1,0:T(8,128)S(1)}, f32[4,32,8,128]{3,2,1,0:T(8,128)S(1)}, u32[]{:S(2)}, u32[]{:S(2)}) collective-permute-start(f32[4,32,8,128]{3,2,1,0:T(8,128)S(1)} %get-tuple-element.143), channel_id=1, source_target_pairs={{1,0},{2,1},{3,2},{4,3},{5,4},{6,5},{7,6},{8,7},{9,8},{10,9},{11,1... | collective-permute-start | bytes 1572872 | tf_op jit(solution)/shard_map/ppermute | solution.py:299
  144.2 18.2 %collective-permute-start.15 = (f32[2,32,8,128]{3,2,1,0:T(8,128)S(1)}, f32[2,32,8,128]{3,2,1,0:T(8,128)S(1)}, u32[]{:S(2)}, u32[]{:S(2)}) collective-permute-start(f32[2,32,8,128]{3,2,1,0:T(8,128)S(1)} %get-tuple-element.172), channel_id=1, source_target_pairs={{0,1},{1,2},{2,3},{3,4},{4,5},{5,6},{6,7},{7,8},{8,9},{9,10},{10,1... | collective-permute-start | bytes 786440 | tf_op jit(solution)/shard_map/ppermute | solution.py:294
  146.1 18.2 %collective-permute-start.18 = (f32[2,32,8,128]{3,2,1,0:T(8,128)S(1)}, f32[2,32,8,128]{3,2,1,0:T(8,128)S(1)}, u32[]{:S(2)}, u32[]{:S(2)}) collective-permute-start(f32[2,32,8,128]{3,2,1,0:T(8,128)S(1)} %get-tuple-element.171), channel_id=1, source_target_pairs={{1,0},{2,1},{3,2},{4,3},{5,4},{6,5},{7,6},{8,7},{9,8},{10,9},{11,1... | collective-permute-start | bytes 786440 | tf_op jit(solution)/shard_map/ppermute | solution.py:299
  153.7 18.2 %collective-permute-start.17 = (f32[2,32,8,128]{3,2,1,0:T(8,128)S(1)}, f32[2,32,8,128]{3,2,1,0:T(8,128)S(1)}, u32[]{:S(2)}, u32[]{:S(2)}) collective-permute-start(f32[2,32,8,128]{3,2,1,0:T(8,128)S(1)} %get-tuple-element.170), channel_id=1, source_target_pairs={{0,1},{1,2},{2,3},{3,4},{4,5},{5,6},{6,7},{7,8},{8,9},{9,10},{10,1... | collective-permute-start | bytes 786440 | tf_op jit(solution)/shard_map/ppermute | solution.py:294
  162.4 11.7 %collective-permute-start.20 = (f32[2,32,8,128]{3,2,1,0:T(8,128)S(1)}, f32[2,32,8,128]{3,2,1,0:T(8,128)S(1)}, u32[]{:S(2)}, u32[]{:S(2)}) collective-permute-start(f32[2,32,8,128]{3,2,1,0:T(8,128)S(1)} %get-tuple-element.169), channel_id=1, source_target_pairs={{1,0},{2,1},{3,2},{4,3},{5,4},{6,5},{7,6},{8,7},{9,8},{10,9},{11,1... | collective-permute-start | bytes 786440 | tf_op jit(solution)/shard_map/ppermute | solution.py:299
  164.3 13.2 %collective-permute-start.24 = (f32[6,48,8,128]{3,2,1,0:T(8,128)S(1)}, f32[6,48,8,128]{3,2,1,0:T(8,128)S(1)}, u32[]{:S(2)}, u32[]{:S(2)}) collective-permute-start(f32[6,48,8,128]{3,2,1,0:T(8,128)S(1)} %pad_maximum_fusion.1), channel_id=1, source_target_pairs={{0,32},{32,0},{64,96},{96,64},{128,160},{160,128},{192,224},{224,1... | collective-permute-start | bytes 3538952 | tf_op jit(solution)/shard_map/ppermute | solution.py:281
  171.9 4.3 %collective-permute-start.23 = (f32[2,48,8,128]{3,2,1,0:T(8,128)S(1)}, f32[2,48,8,128]{3,2,1,0:T(8,128)S(1)}, u32[]{:S(2)}, u32[]{:S(2)}) collective-permute-start(f32[2,48,8,128]{3,2,1,0:T(8,128)S(1)} %constant_dynamic-update-slice_fusion), channel_id=1, source_target_pairs={{0,32},{32,0},{64,96},{96,64},{128,160},{160,128},{192,224},{224,1... | collective-permute-start | bytes 1179656 | tf_op jit(solution)/shard_map/ppermute | solution.py:281
  174.1 3.3 %collective-permute-start.19 = (f32[4,32,8,128]{3,2,1,0:T(8,128)S(1)}, f32[4,32,8,128]{3,2,1,0:T(8,128)S(1)}, u32[]{:S(2)}, u32[]{:S(2)}) collective-permute-start(f32[4,32,8,128]{3,2,1,0:T(8,128)S(1)} %pad_maximum_fusion.3), channel_id=1, source_target_pairs={{0,32},{32,0},{64,96},{96,64},{128,160},{160,128},{192,224},{224,1... | collective-permute-start | bytes 1572872 | tf_op jit(solution)/shard_map/ppermute | solution.py:281
  176.0 3.9 %collective-permute-start.22 = (f32[12,32,8,128]{3,2,1,0:T(8,128)S(1)}, f32[12,32,8,128]{3,2,1,0:T(8,128)S(1)}, u32[]{:S(2)}, u32[]{:S(2)}) collective-permute-start(f32[12,32,8,128]{3,2,1,0:T(8,128)S(1)} %pad_maximum_fusion), channel_id=1, source_target_pairs={{0,32},{32,0},{64,96},{96,64},{128,160},{160,128},{192,224},{224,1... | collective-permute-start | bytes 4718600 | tf_op jit(solution)/shard_map/ppermute | solution.py:281
  190.9 2.4 collective-permute-start.30
  191.3 5.7 %collective-permute-start.25 = (f32[8,24,8,128]{3,2,1,0:T(8,128)S(1)}, f32[8,24,8,128]{3,2,1,0:T(8,128)S(1)}, u32[]{:S(2)}, u32[]{:S(2)}) collective-permute-start(f32[8,24,8,128]{3,2,1,0:T(8,128)S(1)} %get-tuple-element.86), channel_id=1, source_target_pairs={{0,32},{32,0},{64,96},{96,64},{128,160},{160,128},{192,224},{224,1... | collective-permute-start | bytes 2359304 | tf_op jit(solution)/shard_map/ppermute | solution.py:281
  193.4 13.8 %collective-permute-start.31 = (f32[2,24,8,128]{3,2,1,0:T(8,128)S(1)}, f32[2,24,8,128]{3,2,1,0:T(8,128)S(1)}, u32[]{:S(2)}, u32[]{:S(2)}) collective-permute-start(f32[2,24,8,128]{3,2,1,0:T(8,128)S(1)} %get-tuple-element.142), channel_id=1, source_target_pairs={{0,64},{32,96},{64,128},{96,160},{128,192},{160,224},{192,0},{224,... | collective-permute-start | bytes 589832 | tf_op jit(solution)/shard_map/ppermute | solution.py:285
  193.4 16.0 %collective-permute-start.32 = (f32[2,24,8,128]{3,2,1,0:T(8,128)S(1)}, f32[2,24,8,128]{3,2,1,0:T(8,128)S(1)}, u32[]{:S(2)}, u32[]{:S(2)}) collective-permute-start(f32[2,24,8,128]{3,2,1,0:T(8,128)S(1)} %get-tuple-element.141), channel_id=1, source_target_pairs={{0,192},{32,224},{64,0},{96,32},{128,64},{160,96},{192,128},{224,1... | collective-permute-start | bytes 589832 | tf_op jit(solution)/shard_map/ppermute | solution.py:289
  197.1 16.0 %collective-permute-start.26 = (f32[2,24,8,128]{3,2,1,0:T(8,128)S(1)}, f32[2,24,8,128]{3,2,1,0:T(8,128)S(1)}, u32[]{:S(2)}, u32[]{:S(2)}) collective-permute-start(f32[2,24,8,128]{3,2,1,0:T(8,128)S(1)} %get-tuple-element.136), channel_id=1, source_target_pairs={{0,64},{32,96},{64,128},{96,160},{128,192},{160,224},{192,0},{224,... | collective-permute-start | bytes 589832 | tf_op jit(solution)/shard_map/ppermute | solution.py:285
  197.2 17.8 %collective-permute-start.27 = (f32[2,24,8,128]{3,2,1,0:T(8,128)S(1)}, f32[2,24,8,128]{3,2,1,0:T(8,128)S(1)}, u32[]{:S(2)}, u32[]{:S(2)}) collective-permute-start(f32[2,24,8,128]{3,2,1,0:T(8,128)S(1)} %get-tuple-element.135), channel_id=1, source_target_pairs={{0,192},{32,224},{64,0},{96,32},{128,64},{160,96},{192,128},{224,1... | collective-permute-start | bytes 589832 | tf_op jit(solution)/shard_map/ppermute | solution.py:289
  209.4 9.3 %collective-permute-start.33 = (f32[1,24,8,128]{3,2,1,0:T(8,128)S(1)}, f32[1,24,8,128]{3,2,1,0:T(8,128)S(1)}, u32[]{:S(2)}, u32[]{:S(2)}) collective-permute-start(f32[1,24,8,128]{3,2,1,0:T(8,128)S(1)} %get-tuple-element.97), channel_id=1, source_target_pairs={{0,64},{32,96},{64,128},{96,160},{128,192},{160,224},{192,0},{224,... | collective-permute-start | bytes 294920 | tf_op jit(solution)/shard_map/ppermute | solution.py:285
  209.8 9.4 %collective-permute-start.34 = (f32[1,24,8,128]{3,2,1,0:T(8,128)S(1)}, f32[1,24,8,128]{3,2,1,0:T(8,128)S(1)}, u32[]{:S(2)}, u32[]{:S(2)}) collective-permute-start(f32[1,24,8,128]{3,2,1,0:T(8,128)S(1)} %get-tuple-element.98), channel_id=1, source_target_pairs={{0,192},{32,224},{64,0},{96,32},{128,64},{160,96},{192,128},{224,1... | collective-permute-start | bytes 294920 | tf_op jit(solution)/shard_map/ppermute | solution.py:289
  215.1 10.9 %collective-permute-start.28 = (f32[1,24,8,128]{3,2,1,0:T(8,128)S(1)}, f32[1,24,8,128]{3,2,1,0:T(8,128)S(1)}, u32[]{:S(2)}, u32[]{:S(2)}) collective-permute-start(f32[1,24,8,128]{3,2,1,0:T(8,128)S(1)} %get-tuple-element.89), channel_id=1, source_target_pairs={{0,64},{32,96},{64,128},{96,160},{128,192},{160,224},{192,0},{224,... | collective-permute-start | bytes 294920 | tf_op jit(solution)/shard_map/ppermute | solution.py:285
  215.4 10.6 %collective-permute-start.29 = (f32[1,24,8,128]{3,2,1,0:T(8,128)S(1)}, f32[1,24,8,128]{3,2,1,0:T(8,128)S(1)}, u32[]{:S(2)}, u32[]{:S(2)}) collective-permute-start(f32[1,24,8,128]{3,2,1,0:T(8,128)S(1)} %get-tuple-element.90), channel_id=1, source_target_pairs={{0,192},{32,224},{64,0},{96,32},{128,64},{160,96},{192,128},{224,1... | collective-permute-start | bytes 294920 | tf_op jit(solution)/shard_map/ppermute | solution.py:289
  226.2 15.2 %collective-permute-start.35 = (f32[2,48,8,128]{3,2,1,0:T(8,128)S(1)}, f32[2,48,8,128]{3,2,1,0:T(8,128)S(1)}, u32[]{:S(2)}, u32[]{:S(2)}) collective-permute-start(f32[2,48,8,128]{3,2,1,0:T(8,128)S(1)} %fusion.2.refs_7_), channel_id=1, source_target_pairs={{0,64},{32,96},{64,128},{96,160},{128,192},{160,224},{192,0},{224,... | collective-permute-start | bytes 1179656 | tf_op jit(solution)/shard_map/ppermute | solution.py:285
  229.0 12.4 %collective-permute-start.36 = (f32[2,48,8,128]{3,2,1,0:T(8,128)S(1)}, f32[2,48,8,128]{3,2,1,0:T(8,128)S(1)}, u32[]{:S(2)}, u32[]{:S(2)}) collective-permute-start(f32[2,48,8,128]{3,2,1,0:T(8,128)S(1)} %fusion.2.refs_7_), channel_id=1, source_target_pairs={{0,192},{32,224},{64,0},{96,32},{128,64},{160,96},{192,128},{224,1... | collective-permute-start | bytes 1179656 | tf_op jit(solution)/shard_map/ppermute | solution.py:289
  241.4 8.8 %collective-permute-start.37 = (f32[1,48,8,128]{3,2,1,0:T(8,128)S(1)}, f32[1,48,8,128]{3,2,1,0:T(8,128)S(1)}, u32[]{:S(2)}, u32[]{:S(2)}) collective-permute-start(f32[1,48,8,128]{3,2,1,0:T(8,128)S(1)} %get-tuple-element.160.refs_4_), channel_id=1, source_target_pairs={{0,64},{32,96},{64,128},{96,160},{128,192},{160,224},{192,0},{224,... | collective-permute-start | bytes 589832 | tf_op jit(solution)/shard_map/ppermute | solution.py:285
  243.3 16.7 %collective-permute-start.40 = (f32[6,48,8,128]{3,2,1,0:T(8,128)S(1)}, f32[6,48,8,128]{3,2,1,0:T(8,128)S(1)}, u32[]{:S(2)}, u32[]{:S(2)}) collective-permute-start(f32[6,48,8,128]{3,2,1,0:T(8,128)S(1)} %pad_maximum_fusion.2), channel_id=1, source_target_pairs={{0,32},{32,0},{64,96},{96,64},{128,160},{160,128},{192,224},{224,1... | collective-permute-start | bytes 3538952 | tf_op jit(solution)/shard_map/ppermute | solution.py:281
  250.2 7.5 %collective-permute-start.38 = (f32[1,48,8,128]{3,2,1,0:T(8,128)S(1)}, f32[1,48,8,128]{3,2,1,0:T(8,128)S(1)}, u32[]{:S(2)}, u32[]{:S(2)}) collective-permute-start(f32[1,48,8,128]{3,2,1,0:T(8,128)S(1)} %get-tuple-element.162.refs_2_), channel_id=1, source_target_pairs={{0,192},{32,224},{64,0},{96,32},{128,64},{160,96},{192,128},{224,1... | collective-permute-start | bytes 589832 | tf_op jit(solution)/shard_map/ppermute | solution.py:289
  257.7 2.2 collective-permute-start.39
  (15 other events, 75.1 us)
